TPU v7x, 256 devices: a whole 4x4x8 slice. The times are simulated.
256 devices in a mesh: seq: 64 (over y, z, core), head: 4 (over x).
Axes of the slice: x: 4, y: 4, z: 8, core: 2. Of those that a mesh axis runs over, the one named last changes fastest.
Arguments:
- queries: bfloat16 [32768, 2048], P('seq', 'head'), may hold values from -6 to 6
- key_vectors: bfloat16 [32768, 2048], P('seq', 'head'), may hold values from -8 to 8
- value_vectors: bfloat16 [32768, 2048], P('seq', 'head'), may hold values from -40 to 40
- norm_gain: float32 [2048], P('head'), may hold values from 0.25 to 1.75
- out_weight: bfloat16 [2048, 2048], P('head'), may hold values from -0.125 to 0.125
Outputs:
- projected: bfloat16 [32768, 2048], P(('seq', 'head'))
All inputs are finite; a program needn't handle non-finite values.
Results may differ from a plain program's by a relative error of at most 0.013.
Values may be sent and summed in bfloat16 or wider, within the bound.
A program may use at most 128 MiB of HBM per device.

v0:
```python
import math

import jax
import jax.numpy as jnp
from jax import lax
from jax.sharding import Mesh
from jax.sharding import PartitionSpec as P

DH = 128
SEQ = ("seq_0", "seq_1", "seq_2")
SEQ_HEAD = ("seq_0", "seq_1", "seq_2", "head")


highest = lax.Precision.HIGHEST


def filled_with(shard, identity):
    return jnp.zeros_like(shard) + jnp.asarray(identity, shard.dtype)


def prefix_by_axis(shard, axes, combine, identity):
    before = start = filled_with(shard, identity)
    subtotal = shard
    for axis in reversed(axes):
        peers, place = (lax.axis_size(axis), lax.axis_index(axis))
        pieces = lax.all_gather(subtotal.astype(jnp.bfloat16), axis)
        inside, subtotal = (start, start)
        for k in range(peers):
            passed = k < place
            subtotal = combine(subtotal, pieces[k].astype(shard.dtype))
            inside = jnp.where(passed, subtotal, inside)
        before = combine(inside, before)
    return before


def carried_in(shard, axes, combine, identity):
    before = start = filled_with(shard, identity)
    subtotal = shard
    for axis in reversed(axes):
        peers, place = (lax.axis_size(axis), lax.axis_index(axis))
        pieces = lax.all_gather(subtotal, axis)
        inside, subtotal = (start, start)
        for k in range(peers):
            passed = k < place
            subtotal = combine(subtotal, pieces[k])
            inside = jnp.where(passed, subtotal, inside)
        before = combine(inside, before)
    return before


def split_up(shard, dim, peers):
    shape = shard.shape
    parts = shard.reshape(*shape[:dim], peers, shape[dim] // peers, *shape[dim + 1 :])
    return jnp.moveaxis(parts, dim, 0)


def sum_at_owner(shard, axis, dim):
    peers = lax.axis_size(axis)
    parts = lax.all_to_all(split_up(shard, dim, peers), axis, 0, 0, tiled=True)
    return jnp.sum(parts.astype(jnp.float32), axis=0)


def matmul_heads(left_side, right_side):
    return jnp.einsum("hde,hef->hdf", left_side, right_side, precision=highest)


def add_states(earlier, later_part):
    return earlier + later_part


def shards(queries, key_vectors, value_vectors, norm_gain, out_weight):
    token_rows = queries.shape[0]
    head_count = queries.shape[1] // DH
    block_len = math.gcd(token_rows, 256)
    block_count = token_rows // block_len
    query_blocks = queries.reshape(block_count, block_len, head_count, DH)
    key_blocks = key_vectors.reshape(block_count, block_len, head_count, DH)
    value_blocks = value_vectors.reshape(block_count, block_len, head_count, DH)
    position = jnp.arange(block_len)
    lower_mask = (position[None, :] <= position[:, None]).astype(jnp.float32)
    strict_mask = (position[:, None] < position[None, :]).astype(jnp.float32)

    def local_step(carried, block):
        keys_gram, query_value, pair_state = carried
        query_raw, key_raw, value_raw = block
        scores = jnp.einsum("thd,ihd->hti", query_raw, key_raw, preferred_element_type=jnp.float32)
        gram_block = jnp.einsum(
            "thd,the->hde", key_raw, key_raw, preferred_element_type=jnp.float32
        )
        cross_block = jnp.einsum(
            "thd,the->hde", query_raw, value_raw, preferred_element_type=jnp.float32
        )
        query_float = query_raw.astype(jnp.float32)
        key_float = key_raw.astype(jnp.float32)
        value_float = value_raw.astype(jnp.float32)
        paired = jnp.swapaxes(scores, 1, 2) * strict_mask
        inner_pairs = jnp.einsum("hti,hij->htj", scores, paired, precision=highest)
        query_state = jnp.einsum("thd,hde->hte", query_float, keys_gram, precision=highest)
        cross_terms = jnp.einsum("hte,jhe->htj", query_state, query_float, precision=highest)
        mixing = (inner_pairs + cross_terms) * lower_mask
        result = jnp.einsum("htj,jhd->thd", mixing, value_float, precision=highest)
        result = result + jnp.einsum("thd,hde->the", query_float, pair_state, precision=highest)
        paired_values = jnp.einsum("hij,jhe->hie", paired, value_float, precision=highest)
        pair_block = jnp.einsum("ihd,hie->hde", key_float, paired_values, precision=highest)
        pair_next = pair_state + pair_block + matmul_heads(keys_gram, cross_block)
        return (
            (keys_gram + gram_block, query_value + cross_block, pair_next),
            (result, query_value),
        )

    zero_state = jnp.zeros((head_count, DH, DH), jnp.float32)
    device_states, local_parts = lax.scan(
        local_step, (zero_state, zero_state, zero_state), (query_blocks, key_blocks, value_blocks)
    )
    gram_device, cross_device, pair_device = device_states
    local_out, query_value_before = local_parts
    gram_prefix = prefix_by_axis(gram_device, SEQ, add_states, zero_state)
    corrected = pair_device + matmul_heads(gram_prefix, cross_device)
    pair_prefix = carried_in(corrected, SEQ, add_states, zero_state)

    def prefix_step(carried, block):
        query_raw, value_raw, query_value = block
        query_float = query_raw.astype(jnp.float32)
        value_float = value_raw.astype(jnp.float32)
        query_state = jnp.einsum("thd,hde->hte", query_float, gram_prefix, precision=highest)
        cross_terms = (
            jnp.einsum("hte,jhe->htj", query_state, query_float, precision=highest) * lower_mask
        )
        result = jnp.einsum("htj,jhd->thd", cross_terms, value_float, precision=highest)
        result = result + jnp.einsum("thd,hde->the", query_float, pair_prefix, precision=highest)
        result = result + jnp.einsum("hte,hef->thf", query_state, query_value, precision=highest)
        return (carried, result)

    unused, prefix_out = lax.scan(
        prefix_step, jnp.zeros((), jnp.float32), (query_blocks, value_blocks, query_value_before)
    )
    attended = (local_out + prefix_out).reshape(token_rows, head_count, DH)
    mean_square = jnp.mean(attended * attended, axis=-1, keepdims=True)
    normed = attended * lax.rsqrt(mean_square + 1e-06) * norm_gain.reshape(head_count, DH)
    normed = normed.astype(jnp.bfloat16).reshape(token_rows, head_count * DH)
    projected = sum_at_owner(
        jnp.dot(normed, out_weight, preferred_element_type=jnp.float32).astype(jnp.bfloat16),
        "head",
        0,
    )
    return projected.astype(jnp.bfloat16)


def solution(mesh):
    split = Mesh(
        mesh.devices.reshape(4, 8, 2, mesh.shape["head"]), ("seq_0", "seq_1", "seq_2", "head")
    )
    in_specs = (P(SEQ, "head"), P(SEQ, "head"), P(SEQ, "head"), P("head"), P("head", None))
    out_specs = P(SEQ_HEAD, None)
    return jax.shard_map(
        shards, mesh=split, in_specs=in_specs, out_specs=out_specs, check_vma=False
    )
```

profile of v0, /device:TPU:1, one launch (start us, length us, event | category | flops | bytes accessed | tf_op | source)
XLA Modules:
  0.0 240.2 jit_solution(15883175860193404385)
XLA Ops:
  6.6 2.1 reshape.116
  8.7 2.0 reshape.117
  12.7 23.7 %while.31 = (s32[]{:T(128)}, f32[4,128,128]{2,1,0:T(8,128)S(1)}, f32[4,128,128]{2,1,0:T(8,128)S(1)}, f32[4,128,128]{2,1,0:T(8,128)S(1)}, f32[2,256,4,128]{1,3,2,...) while((s32[]{:T(128)}, f32[4,128,128]{2,1,0:T(8,128)S(1)}, ...), condition=%wide.region_1.2_spmd.clone, body=%wide.region_0.1_spmd.clone.sunk | while | flops 2854289408 | bytes 31719652 | solution.py:112
  24.6 1.9 constant_dynamic-slice_fusion.10
  36.5 4.9 %all-gather = bf16[8,128,128]{2,1,0:T(8,128)(2,1)S(1)} all-gather(bf16[4,128,128]{2,1,0:T(8,128)(2,1)S(1)} %convert_element_type.117), channel_id=2, replica_groups=mesh['seq_0'=4,'seq_1'=8,'seq_2'=2,'head'=4] {'seq_2'}, dimensions={0}, use_global_device_ids=true | all-gather | bytes 393216 | tf_op jit(solution)/shard_map/all_gather | solution.py:26
  42.1 34.6 %all-gather.7.cloned.1.call-done = bf16[8,4,128,128]{3,2,1,0:T(8,128)(2,1)} async-done(((bf16[1,4,128,128]{3,2,1,0:T(8,128)(2,1)}), bf16[8,4,128,128]{3,2,1,0:T(8,128)(2,1)}) %all-gather.7.cloned.1.call-update) | async-done | bytes 1048592 | tf_op jit(solution)/shard_map/all_gather | solution.py:26
  78.3 10.2 %all_gather.31 = bf16[4,4,128,128]{3,2,1,0:T(8,128)(2,1)S(1)} all-gather(bf16[1,4,128,128]{3,2,1,0:T(8,128)(2,1)S(1)} %fusion.75), channel_id=1, replica_groups=mesh['seq_0'=4,'seq_1'=8,'seq_2'=2,'head'=4] {'seq_0'}, dimensions={0}, use_global_device_ids=true | all-gather | bytes 655360 | tf_op jit(solution)/shard_map/all_gather | solution.py:26
  90.9 10.5 %all-gather.1 = f32[8,128,128]{2,1,0:T(8,128)S(1)} all-gather(f32[4,128,128]{2,1,0:T(8,128)S(1)} %convolution_add_fusion.3), channel_id=3, replica_groups=mesh['seq_0'=4,'seq_1'=8,'seq_2'=2,'head'=4] {'seq_2'}, dimensions={0}, use_global_device_ids=true | all-gather | bytes 786432 | tf_op jit(solution)/shard_map/all_gather | solution.py:41
  102.4 35.0 %all-gather.11.cloned.1.call-done = f32[32,128,128]{2,1,0:T(8,128)} async-done(((f32[4,128,128]{2,1,0:T(8,128)}), f32[32,128,128]{2,1,0:T(8,128)}) %all-gather.11.cloned.1.call-update) | async-done | bytes 2097168 | tf_op jit(solution)/shard_map/all_gather | solution.py:41
  137.3 2.3 fusion.69
  139.7 28.0 %all-gather.9.cloned.1.call-done = f32[4,4,128,128]{3,2,1,0:T(8,128)} async-done(((f32[1,4,128,128]{3,2,1,0:T(8,128)}), f32[4,4,128,128]{3,2,1,0:T(8,128)}) %all-gather.9.cloned.1.call-update) | async-done | bytes 1048592 | tf_op jit(solution)/shard_map/all_gather | solution.py:41
  167.7 2.7 %fusion.68 = f32[4,128,128]{2,1,0:T(8,128)} fusion(f32[4,4,128,128]{3,2,1,0:T(8,128)} %all-gather.9.cloned.1.call-done, f32[1,4,128,128]{3,2,1,0:T(8,128)} %get-tuple-element.253, f32[4,128,128]{2,1,0:T(8,128)S(1)} %get-tuple-element.254, f32[32,128,128]{2,1,0:T(8,128)} %all-gather.11.cloned.1.call-done, f32[8,128,128]{2,1,0:T(8,128)S(1)} %all-gather.1, ...), kind=kLoop, calls=%fused_computation.99 | loop fusion | flops 1638400 | bytes 3932174 | tf_op jit(solution)/shard_map/add | solution.py:68
  171.5 24.5 %while.30 = (s32[]{:T(128)}, f32[2,256,4,128]{1,3,2,0:T(8,128)}, bf16[2,256,4,128]{3,2,1,0:T(4,128)(2,1)}, bf16[2,256,4,128]{3,2,1,0:T(4,128)(2,1)}, f32[4,128,1...) while((s32[]{:T(128)}, f32[2,256,4,128]{1,3,2,0:T(8,128)}, ...), condition=%wide.region_3.4_spmd.clone, body=%wide.region_2.3_spmd.clone.sunk | while | flops 1409941504 | bytes 10223721 | solution.py:134
  171.5 1.9 constant_dynamic-slice_fusion.8
  174.8 2.4 %convolution_bitcast_fusion.9 = f32[256,4,128]{0,2,1:T(8,128)} fusion(f32[4,256,128]{2,1,0:T(8,128)S(1)} %fusion.128, f32[2,4,128,128]{3,2,1,0:T(8,128)} %get-tuple-element.426, s32[]{:T(128)S(6)} %copy.159), kind=kOutput, calls=%fused_computation.4.clone.1 | convolution fusion | flops 201326592 | bytes 1310724 | tf_op jit(solution)/shard_map/while/body/eval_jaxpr/hte,hef->thf/dot_general | solution.py:131
  177.2 2.2 convolution_bitcast_fusion.10
  181.1 2.7 %fusion.130 = f32[2,256,4,128]{1,3,2,0:T(8,128)} fusion(f32[2,256,4,128]{1,3,2,0:T(8,128)} %get-tuple-element.413, s32[]{:T(128)S(6)} %copy.159, f32[256,4,128]{0,2,1:T(8,128)} %convolution_bitcast_fusion.9, f32[256,4,128]{0,2,1:T(8,128)} %convolution_bitcast_fusion.10, f32[4,256,256]{2,1,0:T(8,128)S(1)} %convolution_multiply_fusion.2, ...), kind=kOutput, calls=%fused_computation.10.clone.1 | convolution fusion | flops 402915328 | bytes 2883588 | tf_op jit(solution)/shard_map/while/body/eval_jaxpr/htj,jhd->thd/dot_general | solution.py:129
  183.8 1.9 constant_dynamic-slice_fusion.8
  187.0 2.4 %convolution_bitcast_fusion.9 = f32[256,4,128]{0,2,1:T(8,128)} fusion(f32[4,256,128]{2,1,0:T(8,128)S(1)} %fusion.128, f32[2,4,128,128]{3,2,1,0:T(8,128)} %get-tuple-element.426, s32[]{:T(128)S(6)} %copy.159), kind=kOutput, calls=%fused_computation.4.clone.1 | convolution fusion | flops 201326592 | bytes 1310724 | tf_op jit(solution)/shard_map/while/body/eval_jaxpr/hte,hef->thf/dot_general | solution.py:131
  189.4 2.2 convolution_bitcast_fusion.10
  193.3 2.7 %fusion.130 = f32[2,256,4,128]{1,3,2,0:T(8,128)} fusion(f32[2,256,4,128]{1,3,2,0:T(8,128)} %get-tuple-element.413, s32[]{:T(128)S(6)} %copy.159, f32[256,4,128]{0,2,1:T(8,128)} %convolution_bitcast_fusion.9, f32[256,4,128]{0,2,1:T(8,128)} %convolution_bitcast_fusion.10, f32[4,256,256]{2,1,0:T(8,128)S(1)} %convolution_multiply_fusion.2, ...), kind=kOutput, calls=%fused_computation.10.clone.1 | convolution fusion | flops 402915328 | bytes 2883588 | tf_op jit(solution)/shard_map/while/body/eval_jaxpr/htj,jhd->thd/dot_general | solution.py:129
  199.9 2.5 %convolution_convert_fusion = bf16[512,2048]{1,0:T(8,128)(2,1)S(1)} fusion(bf16[512,2048]{1,0:T(8,128)(2,1)S(1)} %copy-done, f32[64,8,4,128]{3,2,1,0:T(4,128)S(1)} %bitcast.226, f32[64,8,4,128]{3,2,1,0:T(4,128)} %bitcast.227, f32[512]{0:T(512)S(1)} %copy-done.6), kind=kOutput, calls=%fused_computation.68 | convolution fusion | flops 1075576832 | bytes 6293504 | tf_op jit(solution)/shard_map/dot_general | solution.py:142
  202.4 28.4 %all_to_all.5 = bf16[4,128,2048]{2,1,0:T(8,128)(2,1)} all-to-all(bf16[4,128,2048]{2,1,0:T(8,128)(2,1)S(1)} %bitcast.225), channel_id=1, replica_groups=mesh['seq_0'=4,'seq_1'=8,'seq_2'=2,'head'=4] {'head'}, dimensions={0} | all-to-all | bytes 4194304 | tf_op jit(solution)/shard_map/all_to_all | solution.py:59
  230.8 2.9 %reduce_sum.22 = bf16[128,2048]{1,0:T(8,128)(2,1)} reduce(bf16[4,128,2048]{2,1,0:T(8,128)(2,1)} %all_to_all.5, bf16[]{:T(256)} %constant.65.clone.1), dimensions={0}, to_apply=%region_5.6 | reduce | flops 786432 | bytes 2621442 | tf_op jit(solution)/shard_map/reduce_sum | solution.py:60
  (85 shorter events, 40.2 us)
Async XLA Ops:
  6.5 193.3 %copy-start = (bf16[512,2048]{1,0:T(8,128)(2,1)S(1)}, bf16[512,2048]{1,0:T(8,128)(2,1)}, u32[]{:S(2)}) copy-start(bf16[512,2048]{1,0:T(8,128)(2,1)} %param.13) | copy-start | bytes 6291460
  6.5 4.1 %copy-start.5 = (bf16[512,512]{1,0:T(8,128)(2,1)S(1)}, bf16[512,512]{1,0:T(8,128)(2,1)}, u32[]{:S(2)}) copy-start(bf16[512,512]{1,0:T(8,128)(2,1)} %param.11) | copy-start | bytes 1572868
  6.5 70.2 %all-gather.7.cloned.1.call-start = ((), (), s32[]{:S(2)}) async-start(), calls=%async_computation.1 | async-start | bytes 1179648 | tf_op jit(solution)/shard_map/all_gather | solution.py:26
  15.7 1.0 copy-start.1
  21.6 1.2 copy-start.2
  23.5 1.0 copy-start.3
  27.6 1.0 copy-start.1
  33.5 1.2 copy-start.2
  35.4 1.0 copy-start.3
  42.0 95.3 %all-gather.11.cloned.1.call-start = ((), (), s32[]{:S(2)}) async-start(), calls=%async_computation.3 | async-start | bytes 2359296 | tf_op jit(solution)/shard_map/all_gather | solution.py:41
  76.7 11.8 %copy-start.4 = (bf16[8,4,128,128]{3,2,1,0:T(8,128)(2,1)S(1)}, bf16[8,4,128,128]{3,2,1,0:T(8,128)(2,1)}, u32[]{:S(2)}) copy-start(bf16[8,4,128,128]{3,2,1,0:T(8,128)(2,1)} %all-gather.7.cloned.1.call-done) | copy-start | bytes 3145732
  102.2 65.6 %all-gather.9.cloned.1.call-start = ((), (), s32[]{:S(2)}) async-start(), calls=%async_computation.2 | async-start | bytes 1310720 | tf_op jit(solution)/shard_map/all_gather | solution.py:41
  197.8 2.1 copy-start.6
Sparse Core Ops, SparseCore 0:
  42.2 34.5 all-gather.6
  102.3 35.0 all-gather.10
  139.8 27.8 all-gather.8
where the time goes:
time: 242 us; the launch traced here: 240 us
  waiting for transfers between devices  97.7 us (40%)
  blocking collectives  54 us (22%)
  matrix products  34.5 us (14%)
  local copies, waits for them, and re-layouts  25 us (10%)
  other arithmetic  15.3 us (6%)
  between operations  13.2 us (5%)
    all_gather x2, waiting for transfers between devices, carried_in(): pieces = lax.all_gather(subtotal, axis)  63 us
    all_gather x1, waiting for transfers between devices, prefix_by_axis(): pieces = lax.all_gather(subtotal.astype(jnp.bfloat16), axis)  34.6 us
    all_to_all x1, blocking collectives, sum_at_owner(): parts = lax.all_to_all(split_up(shard, dim, peers), axis, 0, 0, tiled=True)  28.4 us
    all_gather x2, blocking collectives, prefix_by_axis(): pieces = lax.all_gather(subtotal.astype(jnp.bfloat16), axis)  15.1 us
    dynamic_slice x10, local copies, waits for them, and re-layouts, shards(): lax.scan(local_step, (zero_state, zero_state, zero_state), (query_blocks,...  12.2 us
    all_gather x1, blocking collectives, carried_in(): pieces = lax.all_gather(subtotal, axis)  10.5 us
    add x4, other arithmetic, add_states(): return earlier + later_part  6.85 us
    dot_general x2, matrix products, prefix_step(): jnp.einsum('htj,jhd->thd', cross_terms, value_float, precision=highest)  5.43 us
  transfers between devices with their start and end apart: 3, of which 3 were waited for; matrix products, arithmetic and copies ran while one was open for 0% of the time, Pallas kernels for 0%

commit v1 on v0

v1 whole, which is shorter than its diff:
```python
import functools

import jax
import jax.numpy as jnp
from jax import lax
from jax.experimental import pallas as pl
from jax.experimental.pallas import tpu as pltpu
from jax.sharding import Mesh
from jax.sharding import PartitionSpec as P

DH = 128
SEQ = ("seq_0", "seq_1", "seq_2")
SEQ_HEAD = ("seq_0", "seq_1", "seq_2", "head")
F32 = jnp.float32
BF16 = jnp.bfloat16
CHUNK = 256
EPS = 1e-06

X_PIECES = ((-1, 0), (1, 1), (-1, 1), (1, 0), (2, 0), (2, 1))


def dot(a, b, ca, cb):
    return lax.dot_general(a, b, (((ca,), (cb,)), ((), ())), preferred_element_type=F32)


def kernel(
    ny,
    nz,
    nx,
    q_hbm,
    k_hbm,
    v_hbm,
    gain_ref,
    w_hbm,
    out_ref,
    q,
    k,
    v,
    w,
    s_first,
    s_out,
    s_in,
    s_back,
    s_pre,
    p_out,
    p_in,
    p_back,
    p_pre,
    running,
    y_out,
    y_in,
    f_loc,
    p_loc,
    c_loc,
    p_first,
    o_part,
    p_fin,
    n_out,
    n_in,
    acc,
    load_sem,
    z_send,
    z_recv,
    y_send,
    y_recv,
    n_send,
    n_recv,
    w_send,
    w_recv,
):
    tokens, width = q.shape
    heads = width // DH
    group = 2 * nz
    per_head = group // heads if group >= heads else 0
    y, z, c, x = (lax.axis_index(name) for name in SEQ_HEAD)
    me = z * 2 + c

    def modx(i):
        return lax.rem(x + i + nx, nx)

    def mody(i):
        return lax.rem(y + i + ny, ny)

    barrier = pltpu.get_barrier_semaphore()

    def greet_group(d, carry):
        peer = lax.rem(me + d, group)
        pl.semaphore_signal(
            barrier, inc=1, device_id={"seq_1": peer // 2, "seq_2": lax.rem(peer, 2)}, device_id_type=pl.DeviceIdType.MESH
        )
        return carry

    lax.fori_loop(1, group, greet_group, 0)
    for d in range(1, ny):
        pl.semaphore_signal(barrier, inc=1, device_id={"seq_0": mody(d)}, device_id_type=pl.DeviceIdType.MESH)
    for d in range(1, nx):
        pl.semaphore_signal(barrier, inc=1, device_id={"head": modx(d)}, device_id_type=pl.DeviceIdType.MESH)

    loads = [
        pltpu.make_async_copy(src, dst, load_sem.at[i])
        for i, (src, dst) in enumerate(((k_hbm, k), (q_hbm, q), (v_hbm, v), (w_hbm, w.at[x])))
    ]
    for copy in loads:
        copy.start()

    def chunk(ref, h, j):
        return ref[j * CHUNK : (j + 1) * CHUNK, h * DH : (h + 1) * DH]

    def head_state(ref, h):
        rows = ref.shape[1]
        n = DH // rows
        return ref[h * n : (h + 1) * n].reshape(DH, DH)

    def set_head_state(ref, h, value):
        rows = ref.shape[1]
        n = DH // rows
        ref[h * n : (h + 1) * n] = value.reshape(n, rows, DH).astype(ref.dtype)

    def exchange(phase, src, dst, peer, slot):
        return pltpu.make_async_remote_copy(
            src_ref=src.at[peer],
            dst_ref=dst.at[slot],
            send_sem=z_send.at[phase, peer],
            recv_sem=z_recv.at[phase, slot],
            device_id={"seq_1": peer // 2, "seq_2": lax.rem(peer, 2)},
            device_id_type=pl.DeviceIdType.MESH,
        )

    def exchange_start(phase, src, dst):
        def step(d, carry):
            exchange(phase, src, dst, lax.rem(me + d, group), me).start()
            return carry

        lax.fori_loop(1, group, step, 0)
        dst[me] = src[me]

    def exchange_wait(phase, src, dst):
        def step(d, carry):
            peer = lax.rem(me + d, group)
            exchange(phase, src, dst, peer, peer).wait_recv()
            return carry

        lax.fori_loop(1, group, step, 0)

    def exchange_drain(phase, src, dst):
        def step(d, carry):
            peer = lax.rem(me + d, group)
            exchange(phase, src, dst, peer, peer).wait_send()
            return carry

        lax.fori_loop(1, group, step, 0)

    def total_copy(which, d, slot):
        return pltpu.make_async_remote_copy(
            src_ref=y_out.at[which],
            dst_ref=y_in.at[which, slot],
            send_sem=y_send.at[which, d],
            recv_sem=y_recv.at[which, slot],
            device_id={"seq_0": mody(d)},
            device_id_type=pl.DeviceIdType.MESH,
        )

    def scan_totals(which, arrived):
        total = jnp.zeros(arrived.shape[1:], F32)
        for r in range(group):
            running[r] = total
            total = total + arrived[r].astype(F32)
        y_out[which] = total.astype(BF16)
        for d in range(1, ny):
            total_copy(which, d, y).start()

    def scan_finish(which, prefixes):
        base = jnp.zeros(running.shape[1:], F32)
        for d in range(1, ny):
            other = mody(d)
            total_copy(which, d, other).wait_recv()
            base = base + jnp.where(other < y, y_in[which, other].astype(F32), 0.0)
        for r in range(group):
            prefixes[r] = (running[r] + base).astype(BF16)

    colour = lax.rem(y, 2)
    piece_rows = w.shape[1] // 8

    def piece(i, colour_of, core_of):
        offset, half = X_PIECES[i]
        start = colour_of * (4 * piece_rows) + core_of * (2 * piece_rows) + half * piece_rows
        return w.at[modx(offset), pl.ds(pl.multiple_of(start, piece_rows), piece_rows)]

    def w_copy(number, src, dst, device_id):
        return pltpu.make_async_remote_copy(
            src_ref=src,
            dst_ref=dst,
            send_sem=w_send.at[number],
            recv_sem=w_recv.at[number],
            device_id=device_id,
            device_id_type=pl.DeviceIdType.MESH,
        )

    def own_piece(half):
        start = colour * (4 * piece_rows) + c * (2 * piece_rows) + half * piece_rows
        rows = pl.ds(pl.multiple_of(start, piece_rows), piece_rows)
        return w_hbm.at[rows], w.at[x, rows]

    def x_send(number):
        offset, half = X_PIECES[number]
        if number < 4:
            src, dst = own_piece(half)
            return w_copy(number, src, dst, {"head": modx(-offset)})
        src = piece(0 if number == 4 else 1, colour, c)
        return w_copy(number, src, src, {"head": modx(1 if number == 4 else -1)})

    def x_arrival(number):
        ref = piece(number, colour, c)
        return w_copy(number, ref, ref, {"head": modx(1)})

    def core_send(number):
        ref = piece(number, colour, c)
        return w_copy(6 + number, ref, ref, {"seq_2": 1 - c})

    def core_arrival(number):
        ref = piece(number, colour, 1 - c)
        return w_copy(6 + number, ref, ref, {"seq_2": 1 - c})

    def y_step(number):
        return 1 if X_PIECES[number][1] == 0 else -1

    def y_piece_send(number):
        ref = piece(number, colour, c)
        return w_copy(12 + number, ref, ref, {"seq_0": mody(y_step(number))})

    def y_piece_arrival(number):
        ref = piece(number, 1 - colour, c)
        return w_copy(12 + number, ref, ref, {"seq_0": mody(y_step(number))})

    def core2_send(number):
        ref = piece(number, 1 - colour, c)
        return w_copy(18 + number, ref, ref, {"seq_2": 1 - c})

    def core2_arrival(number):
        ref = piece(number, 1 - colour, 1 - c)
        return w_copy(18 + number, ref, ref, {"seq_2": 1 - c})

    def relay_x(numbers):
        for number in numbers:
            x_arrival(number).wait_recv()
            if number < 2:
                x_send(4 + number).start()
            y_piece_send(number).start()
            core_send(number).start()

    def relay_y(numbers):
        for number in numbers:
            y_piece_arrival(number).wait_recv()
            core2_send(number).start()

    loads[0].wait()
    for h in range(heads):
        first = dot(chunk(k, h, 0), chunk(k, h, 0), 0, 0)
        s_first[h] = first.astype(BF16)
        set_head_state(s_out, h, first + dot(chunk(k, h, 1), chunk(k, h, 1), 0, 0))

    pl.semaphore_wait(barrier, group - 1 + ny - 1 + nx - 1)
    exchange_start(0, s_out, s_in)
    for number in range(4):
        x_send(number).start()
    loads[1].wait()
    loads[2].wait()

    row = lax.broadcasted_iota(jnp.int32, (CHUNK, CHUNK), 0)
    col = lax.broadcasted_iota(jnp.int32, (CHUNK, CHUNK), 1)

    def local_pairs(h):
        pair = jnp.zeros((DH, DH), F32)
        cross = jnp.zeros((DH, DH), F32)
        for j in range(2):
            qc, kc, vc = chunk(q, h, j), chunk(k, h, j), chunk(v, h, j)
            scores = jnp.where(col < row, dot(qc, kc, 1, 1), 0.0).astype(BF16)
            f = dot(scores, kc, 1, 0)
            if j == 1:
                f = f + dot(qc, s_first[h], 1, 0)
            f_loc[j * CHUNK : (j + 1) * CHUNK, h * DH : (h + 1) * DH] = f
            pair = pair + dot(f.astype(BF16), vc, 0, 0)
            cross = cross + dot(qc, vc, 0, 0)
        p_loc[h] = pair
        c_loc[h] = cross.astype(BF16)

    def local_out(h):
        s_h = head_state(s_pre, h)
        for j in range(2):
            qc, vc = chunk(q, h, j), chunk(v, h, j)
            f = (chunk(f_loc, h, j) + dot(qc, s_h, 1, 0)).astype(BF16)
            mixing = jnp.where(col <= row, dot(qc, f, 1, 1), 0.0).astype(BF16)
            o_part[j * CHUNK : (j + 1) * CHUNK, h * DH : (h + 1) * DH] = dot(mixing, vc, 1, 0)
            if j == 0:
                p_first[h] = dot(f, vc, 0, 0)

    for h in range(heads):
        local_pairs(h)

    exchange_wait(0, s_out, s_in)
    scan_totals(0, s_in)
    scan_finish(0, s_back)
    exchange_start(1, s_back, s_pre)
    exchange_wait(1, s_back, s_pre)

    for h in range(heads):
        set_head_state(p_out, h, p_loc[h] + dot(head_state(s_pre, h), c_loc[h], 1, 0))
    exchange_start(2, p_out, p_in)
    relay_x((0, 1))
    for h in range(heads // 2):
        local_out(h)
    exchange_wait(2, p_out, p_in)
    scan_totals(1, p_in)
    scan_finish(1, p_back)
    exchange_start(3, p_back, p_pre)
    relay_x((2, 3))
    relay_y((0, 1))
    for h in range(heads // 2, heads):
        local_out(h)
    exchange_wait(3, p_back, p_pre)
    for h in range(heads):
        p_h = head_state(p_pre, h)
        p_fin[0, h] = p_h
        p_fin[1, h] = (p_h.astype(F32) + p_first[h]).astype(BF16)

    rows_x = tokens // nx

    def n_copy(d, slot):
        return pltpu.make_async_remote_copy(
            src_ref=n_out.at[d],
            dst_ref=n_in.at[slot],
            send_sem=n_send.at[d],
            recv_sem=n_recv.at[slot],
            device_id={"head": modx(d)},
            device_id_type=pl.DeviceIdType.MESH,
        )

    for d in (2, 1, 3, 0):
        target = modx(d)
        rows = pl.ds(pl.multiple_of(target * rows_x, rows_x), rows_x)
        part = target // (CHUNK // rows_x)
        for h in range(heads):
            cols = slice(h * DH, (h + 1) * DH)
            attended = o_part[rows, cols] + dot(q[rows, cols], p_fin[part, h], 1, 0)
            mean_square = jnp.mean(attended * attended, axis=-1, keepdims=True)
            n_out[d, :, cols] = (attended * lax.rsqrt(mean_square + EPS) * gain_ref[:, cols]).astype(BF16)
        if d:
            n_copy(d, x).start()
    relay_x((4, 5))
    relay_y((2, 3))

    loads[3].wait()
    tile = 512
    n_cols = out_ref.shape[1]

    def project(rows_in, quarter, first, last):
        for start in range(0, n_cols, tile):
            cols = slice(start, start + tile)
            part = dot(rows_in, w[quarter, :, cols], 1, 0)
            if not first:
                part = part + acc[:, cols]
            if last:
                out_ref[:, cols] = part.astype(BF16)
            else:
                acc[:, cols] = part

    project(n_out[0], x, True, False)
    relay_y((4, 5))
    for offset in (-1, 1, 2):
        quarter = modx(offset)
        for number, (of, half) in enumerate(X_PIECES):
            if of == offset:
                core_arrival(number).wait_recv()
                core2_arrival(number).wait_recv()
        n_copy(offset % nx, quarter).wait_recv()
        project(n_in[quarter], quarter, False, offset == 2)

    exchange_drain(0, s_out, s_in)
    exchange_drain(1, s_back, s_pre)
    exchange_drain(2, p_out, p_in)
    exchange_drain(3, p_back, p_pre)
    for which in range(2):
        for d in range(1, ny):
            total_copy(which, d, y).wait_send()
    for d in range(1, nx):
        n_copy(d, x).wait_send()
    for number in range(6):
        x_send(number).wait_send()
        core_send(number).wait_send()
        y_piece_send(number).wait_send()
        core2_send(number).wait_send()


def shards(ny, nz, nx, queries, key_vectors, value_vectors, norm_gain, out_weight):
    tokens, width = queries.shape
    heads = width // DH
    depth, n_cols = out_weight.shape
    group = 2 * nz
    rows = heads * DH // group
    state = pltpu.VMEM((group, rows, DH), BF16)
    matrices = (heads, DH, DH)
    any_spec = pl.BlockSpec(memory_space=pl.ANY)
    vmem_spec = pl.BlockSpec(memory_space=pltpu.VMEM)
    return pl.pallas_call(
        functools.partial(kernel, ny, nz, nx),
        out_shape=jax.ShapeDtypeStruct((tokens // nx, n_cols), BF16),
        in_specs=[any_spec, any_spec, any_spec, vmem_spec, any_spec],
        out_specs=vmem_spec,
        scratch_shapes=[
            pltpu.VMEM((tokens, width), BF16),
            pltpu.VMEM((tokens, width), BF16),
            pltpu.VMEM((tokens, width), BF16),
            pltpu.VMEM((nx, depth, n_cols), BF16),
            pltpu.VMEM(matrices, BF16),
            state,
            state,
            state,
            state,
            state,
            state,
            state,
            state,
            pltpu.VMEM((group, rows, DH), F32),
            pltpu.VMEM((2, rows, DH), BF16),
            pltpu.VMEM((2, ny, rows, DH), BF16),
            pltpu.VMEM((tokens, width), F32),
            pltpu.VMEM(matrices, F32),
            pltpu.VMEM(matrices, BF16),
            pltpu.VMEM(matrices, F32),
            pltpu.VMEM((tokens, width), F32),
            pltpu.VMEM((2,) + matrices, BF16),
            pltpu.VMEM((nx, tokens // nx, width), BF16),
            pltpu.VMEM((nx, tokens // nx, width), BF16),
            pltpu.VMEM((tokens // nx, n_cols), F32),
            pltpu.SemaphoreType.DMA((4,)),
            pltpu.SemaphoreType.DMA((4, group)),
            pltpu.SemaphoreType.DMA((4, group)),
            pltpu.SemaphoreType.DMA((2, ny)),
            pltpu.SemaphoreType.DMA((2, ny)),
            pltpu.SemaphoreType.DMA((nx,)),
            pltpu.SemaphoreType.DMA((nx,)),
            pltpu.SemaphoreType.DMA((24,)),
            pltpu.SemaphoreType.DMA((24,)),
        ],
        compiler_params=pltpu.CompilerParams(
            collective_id=0, has_side_effects=True, vmem_limit_bytes=48 * 1024 * 1024
        ),
    )(queries, key_vectors, value_vectors, norm_gain.reshape(1, width), out_weight)


def solution(mesh):
    seq, nx = mesh.shape["seq"], mesh.shape["head"]
    ny = 4 if seq == 64 else 2
    nz = seq // (2 * ny)
    split = Mesh(mesh.devices.reshape(ny, nz, 2, nx), SEQ_HEAD)
    in_specs = (P(SEQ, "head"), P(SEQ, "head"), P(SEQ, "head"), P("head"), P("head", None))
    out_specs = P(SEQ_HEAD, None)
    return jax.shard_map(
        functools.partial(shards, ny, nz, nx), mesh=split, in_specs=in_specs, out_specs=out_specs, check_vma=False
    )
```

time: 242 us -> 61.9 us (0.26)
  waiting for transfers between devices: 97.7 us -> 0 us
  Pallas kernels: 0 us -> 54.6 us
  blocking collectives: 54 us -> 0 us
  matrix products: 34.5 us -> 0 us
  local copies, waits for them, and re-layouts: 25 us -> 6.19 us
  other arithmetic: 15.3 us -> 0 us
  between operations: 13.2 us -> 0.01 us
    all_gather x3 -> x0, waiting for transfers between devices: 97.6 us -> none  [the longest x2 63 us: carried_in(): pieces = lax.all_gather(subtotal, axis)]
    pallas_call x0 -> x1, Pallas kernels: none -> 54.6 us  [shards(): pl.pallas_call(functools.partial(kernel, ny, nz, nx), out_shape=jax.Shape...]
    dot_general x34 -> x0, matrix products: 34.5 us -> none  [the longest x2 5.43 us: prefix_step(): jnp.einsum('htj,jhd->thd', cross_terms, value_float, precision=highest)]
    all_to_all x1 -> x0, blocking collectives: 28.4 us -> none  [sum_at_owner(): parts = lax.all_to_all(split_up(shard, dim, peers), axis, 0, 0, tiled=True)]
    all_gather x3 -> x0, blocking collectives: 25.6 us -> none  [the longest x2 15.1 us: prefix_by_axis(): pieces = lax.all_gather(subtotal.astype(jnp.bfloat16), axis)]
    dynamic_slice x10 -> x0, local copies, waits for them, and re-layouts: 12.2 us -> none  [shards(): lax.scan(local_step, (zero_state, zero_state, zero_state), (query_blocks,...]
    add x4 -> x0, other arithmetic: 6.85 us -> none  [add_states(): return earlier + later_part]
    unnamed x8 -> x11, local copies, waits for them, and re-layouts: 0.02 us -> 6.19 us
  transfers between devices with their start and end apart: 3 -> 0, of which waited for: 3 -> 0; matrix products, arithmetic and copies ran while one was open for 0% -> 0% of each run, Pallas kernels for 0% -> 0%
where the time goes in v1:
time: 61.9 us; the launch traced here: 60.8 us
  Pallas kernels  54.6 us (88%)
  local copies, waits for them, and re-layouts  6.19 us (10%)
    pallas_call x1, Pallas kernels, shards(): pl.pallas_call(functools.partial(kernel, ny, nz, nx), out_shape=jax.Shape...  54.6 us
    unnamed x11, local copies, waits for them, and re-layouts  6.19 us

profile of v1, /device:TPU:1, one launch (start us, length us, event | category | flops | bytes accessed | tf_op | source)
XLA Modules:
  0.0 60.8 jit_solution(11230563277759506402)
XLA Ops:
  0.0 0.0 copy-start
  0.0 1.6 %copy-done = bf16[512,2048]{1,0:T(8,128)(2,1)S(1)} copy-done((bf16[512,2048]{1,0:T(8,128)(2,1)S(1)}, bf16[512,2048]{1,0:T(8,128)(2,1)}, u32[]{:S(2)}) %copy-start) | copy-done | bytes 2097176
  1.6 0.0 copy-start.1
  1.6 1.0 %copy-done.1 = bf16[512,512]{1,0:T(8,128)(2,1)S(1)} copy-done((bf16[512,512]{1,0:T(8,128)(2,1)S(1)}, bf16[512,512]{1,0:T(8,128)(2,1)}, u32[]{:S(2)}) %copy-start.1) | copy-done | bytes 524312
  2.6 0.0 copy-start.2
  2.6 1.0 %copy-done.2 = bf16[512,512]{1,0:T(8,128)(2,1)S(1)} copy-done((bf16[512,512]{1,0:T(8,128)(2,1)S(1)}, bf16[512,512]{1,0:T(8,128)(2,1)}, u32[]{:S(2)}) %copy-start.2) | copy-done | bytes 524312
  3.7 0.0 copy-start.3
  3.7 1.0 %copy-done.3 = bf16[512,512]{1,0:T(8,128)(2,1)S(1)} copy-done((bf16[512,512]{1,0:T(8,128)(2,1)S(1)}, bf16[512,512]{1,0:T(8,128)(2,1)}, u32[]{:S(2)}) %copy-start.3) | copy-done | bytes 524312
  4.7 0.0 copy-start.4
  4.7 0.7 %copy-done.4 = f32[512]{0:T(512)S(1)} copy-done((f32[512]{0:T(512)S(1)}, f32[512]{0:T(512)}, u32[]{:S(2)}) %copy-start.4) | copy-done | bytes 2072
  5.4 54.6 %shard_map.55 = bf16[128,2048]{1,0:T(8,128)(2,1)S(1)} custom-call(bf16[512,512]{1,0:T(8,128)(2,1)S(1)} %copy-done.1, bf16[512,512]{1,0:T(8,128)(2,1)S(1)} %copy-done.2, bf16[512,512]{1,0:T(8,128)(2,1)S(1)} %copy-done.3, f32[1,512]{1,0:T(1,128)S(1)} %bitcast.1, bf16[512,2048]{1,0:T(8,128)(2,1)S(1)} %copy-done), custom_call_target="tpu_custom_call" | custom-call | tf_op jit(solution)/shard_map/pallas_call | solution.py:404
  60.0 0.8 %copy.7 = bf16[128,2048]{1,0:T(8,128)(2,1)} copy(bf16[128,2048]{1,0:T(8,128)(2,1)S(1)} %shard_map.55) | data formatting | bytes 1048576
Async XLA Ops:
  0.0 1.6 %copy-start = (bf16[512,2048]{1,0:T(8,128)(2,1)S(1)}, bf16[512,2048]{1,0:T(8,128)(2,1)}, u32[]{:S(2)}) copy-start(bf16[512,2048]{1,0:T(8,128)(2,1)} %w_hbm.1) | copy-start | bytes 6291460
  1.6 1.0 %copy-start.1 = (bf16[512,512]{1,0:T(8,128)(2,1)S(1)}, bf16[512,512]{1,0:T(8,128)(2,1)}, u32[]{:S(2)}) copy-start(bf16[512,512]{1,0:T(8,128)(2,1)} %q_hbm.1) | copy-start | bytes 1572868
  2.6 1.0 %copy-start.2 = (bf16[512,512]{1,0:T(8,128)(2,1)S(1)}, bf16[512,512]{1,0:T(8,128)(2,1)}, u32[]{:S(2)}) copy-start(bf16[512,512]{1,0:T(8,128)(2,1)} %k_hbm.1) | copy-start | bytes 1572868
  3.7 1.0 %copy-start.3 = (bf16[512,512]{1,0:T(8,128)(2,1)S(1)}, bf16[512,512]{1,0:T(8,128)(2,1)}, u32[]{:S(2)}) copy-start(bf16[512,512]{1,0:T(8,128)(2,1)} %v_hbm.1) | copy-start | bytes 1572868
  4.7 0.7 %copy-start.4 = (f32[512]{0:T(512)S(1)}, f32[512]{0:T(512)}, u32[]{:S(2)}) copy-start(f32[512]{0:T(512)} %param.8) | copy-start | bytes 6148

commit v2 on v1

v2 whole, which is shorter than its diff:
```python
import functools

import jax
import jax.numpy as jnp
from jax import lax
from jax.experimental import pallas as pl
from jax.experimental.pallas import tpu as pltpu
from jax.sharding import Mesh
from jax.sharding import PartitionSpec as P

DH = 128
SEQ = ("seq_0", "seq_1", "seq_2")
SEQ_HEAD = ("seq_0", "seq_1", "seq_2", "head")
F32 = jnp.float32
BF16 = jnp.bfloat16
CHUNK = 256
EPS = 1e-06
FAR_FIRST = (4, 3, 5, 2, 6, 1, 7)

X_PIECES = ((-1, 0), (1, 1), (-1, 1), (1, 0), (2, 0), (2, 1))


def dot(a, b, ca, cb):
    return lax.dot_general(a, b, (((ca,), (cb,)), ((), ())), preferred_element_type=F32)


def kernel(
    ny,
    nz,
    nx,
    q_hbm,
    k_hbm,
    v_hbm,
    gain_hbm,
    w_hbm,
    out_ref,
    q,
    k,
    v,
    w,
    gain,
    s_first,
    s_loc,
    cp_loc,
    s_sib,
    cp_sib,
    s_chip,
    cp_chip,
    s_arr,
    cp_arr,
    running,
    s_back,
    p_back,
    y_out,
    y_in,
    s_pre,
    p_pre,
    p_step,
    s_other,
    p_other,
    s_mine,
    p_mine,
    f_loc,
    p_first,
    o_part,
    p_fin,
    n_out,
    n_in,
    acc,
    load_sem,
    core_send,
    core_recv,
    in_send,
    in_recv,
    back_send,
    back_recv,
    y_send,
    y_recv,
    n_send,
    n_recv,
    w_send,
    w_recv,
):
    tokens, width = q.shape
    heads = width // DH
    pair = heads // 2
    y, z, c, x = (lax.axis_index(name) for name in SEQ_HEAD)

    def modx(i):
        return lax.rem(x + i + nx, nx)

    def mody(i):
        return lax.rem(y + i + ny, ny)

    def modz(i):
        return lax.rem(z + i, nz)

    pending = []

    def remote(src, dst, send_sem, recv_sem, device_id):
        return pltpu.make_async_remote_copy(
            src_ref=src,
            dst_ref=dst,
            send_sem=send_sem,
            recv_sem=recv_sem,
            device_id=device_id,
            device_id_type=pl.DeviceIdType.MESH,
        )

    def start(copy):
        copy.start()
        pending.append(copy.wait_send)

    barrier = pltpu.get_barrier_semaphore()
    greeted = [{"seq_1": modz(d)} for d in range(1, nz)] + [{"seq_2": 1 - c}]
    greeted += [{"seq_0": mody(d)} for d in range(1, ny)] + [{"head": modx(d)} for d in range(1, nx)]
    for peer in greeted:
        pl.semaphore_signal(barrier, inc=1, device_id=peer, device_id_type=pl.DeviceIdType.MESH)

    loads = [
        pltpu.make_async_copy(src, dst, load_sem.at[i])
        for i, (src, dst) in enumerate(((k_hbm, k), (q_hbm, q), (v_hbm, v), (w_hbm, w.at[x]), (gain_hbm, gain)))
    ]
    for copy in loads:
        copy.start()

    def chunk(ref, h, j):
        return ref[j * CHUNK : (j + 1) * CHUNK, h * DH : (h + 1) * DH]

    spacing = nz // heads
    is_worker = (lax.rem(z, spacing) == 0) & (z // (spacing * pair) == c)
    my_head = lax.rem(z // spacing, pair)

    def worker_z(i):
        return (c * pair + i) * spacing

    def in_copy(kind, i, slot, device_id):
        src, dst = ((s_chip, s_arr), (cp_chip, cp_arr))[kind]
        return remote(src.at[i], dst.at[slot], in_send.at[kind, i], in_recv.at[kind, slot], device_id)

    def send_in(kind):
        for i in range(pair):
            here = z == worker_z(i)
            copy = in_copy(kind, i, z, {"seq_1": worker_z(i)})

            @pl.when(jnp.logical_not(here))
            def _(copy=copy):
                copy.start()

            @pl.when(here)
            def _(i=i):
                src, dst = ((s_chip, s_arr), (cp_chip, cp_arr))[kind]
                dst[z] = src[i]

    def drain_in(kind):
        for i in range(pair):
            @pl.when(z != worker_z(i))
            def _(i=i):
                in_copy(kind, i, z, {"seq_1": worker_z(i)}).wait_send()

    def wait_in(kind):
        for d in range(1, nz):
            in_copy(kind, 0, modz(d), {"seq_1": modz(d)}).wait_recv()

    def back_copy(kind, i, d):
        src, dst = ((s_back, s_pre), (p_back, p_pre))[kind]
        return remote(src.at[modz(d)], dst.at[i], back_send.at[kind, d], back_recv.at[kind, i], {"seq_1": modz(d)})

    def send_back(kind):
        src, dst = ((s_back, s_pre), (p_back, p_pre))[kind]
        for d in FAR_FIRST:
            if d < nz:
                back_copy(kind, my_head, d).start()
        dst[my_head] = src[z]

    def wait_back(kind):
        for i in range(pair):
            @pl.when(z != worker_z(i))
            def _(i=i):
                back_copy(kind, i, 1).wait_recv()

    def total_copy(kind, d, slot):
        return remote(
            y_out.at[kind], y_in.at[kind, slot], y_send.at[kind, d], y_recv.at[kind, slot], {"seq_0": mody(d)}
        )

    def send_total(kind, total):
        y_out[kind] = total.astype(BF16)
        for d in range(1, ny):
            total_copy(kind, d, y).start()

    def wait_totals(kind):
        base = jnp.zeros((DH, DH), F32)
        for d in range(1, ny):
            other = mody(d)
            total_copy(kind, d, other).wait_recv()
            base = base + jnp.where(other < y, y_in[kind, other].astype(F32), 0.0)
        return base

    colour = lax.rem(y, 2)
    piece_rows = w.shape[1] // 8

    def rows_of(colour_of, core_of, half):
        first = colour_of * (4 * piece_rows) + core_of * (2 * piece_rows) + half * piece_rows
        return pl.ds(pl.multiple_of(first, piece_rows), piece_rows)

    def piece(i, colour_of, core_of):
        offset, half = X_PIECES[i]
        return w.at[modx(offset), rows_of(colour_of, core_of, half)]

    def w_copy(number, src, dst, device_id):
        return remote(src, dst, w_send.at[number], w_recv.at[number], device_id)

    def x_send(number):
        offset, half = X_PIECES[number]
        if number < 4:
            rows = rows_of(colour, c, half)
            return w_copy(number, w_hbm.at[rows], w.at[x, rows], {"head": modx(-offset)})
        src = piece(number - 4, colour, c)
        return w_copy(number, src, src, {"head": modx(1 if number == 4 else -1)})

    def x_arrival(number):
        ref = piece(number, colour, c)
        return w_copy(number, ref, ref, {"head": modx(1)})

    def core_copy(number, core_of):
        ref = piece(number, colour, core_of)
        return w_copy(6 + number, ref, ref, {"seq_2": 1 - c})

    def y_copy(number, colour_of):
        ref = piece(number, colour_of, c)
        return w_copy(12 + number, ref, ref, {"seq_0": mody(1 if X_PIECES[number][1] == 0 else -1)})

    def core_y_copy(number, core_of):
        ref = piece(number, 1 - colour, core_of)
        return w_copy(18 + number, ref, ref, {"seq_2": 1 - c})

    def relay_x(numbers):
        for number in numbers:
            x_arrival(number).wait_recv()
            if number < 2:
                start(x_send(4 + number))
            start(y_copy(number, colour))
            start(core_copy(number, c))

    def relay_y(numbers):
        for number in numbers:
            y_copy(number, 1 - colour).wait_recv()
            start(core_y_copy(number, c))

    row = lax.broadcasted_iota(jnp.int32, (CHUNK, CHUNK), 0)
    col = lax.broadcasted_iota(jnp.int32, (CHUNK, CHUNK), 1)
    loads[0].wait()
    for h in range(heads):
        first = dot(chunk(k, h, 0), chunk(k, h, 0), 0, 0)
        s_first[h] = first.astype(BF16)
        s_loc[h // pair, h % pair] = (first + dot(chunk(k, h, 1), chunk(k, h, 1), 0, 0)).astype(BF16)
    loads[1].wait()
    loads[2].wait()
    for h in range(heads):
        pairs = jnp.zeros((DH, DH), F32)
        cross = jnp.zeros((DH, DH), F32)
        for j in range(2):
            qc, kc, vc = chunk(q, h, j), chunk(k, h, j), chunk(v, h, j)
            scores = jnp.where(col < row, dot(qc, kc, 1, 1), 0.0).astype(BF16)
            f = dot(scores, kc, 1, 0)
            if j == 1:
                f = f + dot(qc, s_first[h], 1, 0)
            f_loc[j * CHUNK : (j + 1) * CHUNK, h * DH : (h + 1) * DH] = f
            pairs = pairs + dot(f.astype(BF16), vc, 0, 0)
            cross = cross + dot(qc, vc, 0, 0)
        cp_loc[h // pair, h % pair, 0] = cross.astype(BF16)
        cp_loc[h // pair, h % pair, 1] = pairs.astype(BF16)

    pl.semaphore_wait(barrier, len(greeted))
    sibling = {"seq_2": 1 - c}
    s_core = remote(s_loc.at[1 - c], s_sib, core_send.at[0], core_recv.at[0], sibling)
    cp_core = remote(cp_loc.at[1 - c], cp_sib, core_send.at[1], core_recv.at[1], sibling)
    start(s_core)
    start(cp_core)
    for number in range(4):
        start(x_send(number))
    s_core.wait_recv()
    for i in range(pair):
        s_chip[i] = (s_loc[c, i].astype(F32) + s_sib[i].astype(F32)).astype(BF16)
    send_in(0)
    cp_core.wait_recv()
    for i in range(pair):
        mine, other = cp_loc[c, i], cp_sib[i]
        early = jnp.where(c == 0, s_loc[c, i], s_sib[i])
        late = jnp.where(c == 0, other[0], mine[0])
        cp_chip[i, 0] = (mine[0].astype(F32) + other[0].astype(F32)).astype(BF16)
        cp_chip[i, 1] = (mine[1].astype(F32) + other[1].astype(F32) + dot(early, late, 1, 0)).astype(BF16)
    send_in(1)

    @pl.when(is_worker)
    def _():
        wait_in(0)
        total = jnp.zeros((DH, DH), F32)
        for r in range(nz):
            running[r] = total
            total = total + s_arr[r].astype(F32)
        send_total(0, total)

    relay_x((0, 1))

    @pl.when(is_worker)
    def _():
        base = wait_totals(0)
        for r in range(nz):
            s_back[r] = (running[r] + base).astype(BF16)
        send_back(0)
        wait_in(1)
        total = jnp.zeros((DH, DH), F32)
        for r in range(nz):
            running[r] = total
            total = total + cp_arr[r, 1].astype(F32) + dot(s_back[r], cp_arr[r, 0], 1, 0)
        send_total(1, total)

    relay_x((2, 3))
    relay_y((0, 1))

    @pl.when(is_worker)
    def _():
        base = wait_totals(1)
        for r in range(nz):
            p_back[r] = (running[r] + base).astype(BF16)
        send_back(1)

    wait_back(0)
    for i in range(pair):
        mine, other = cp_loc[c, i], cp_sib[i]
        chip = s_pre[i]
        early = jnp.where(c == 0, s_loc[c, i], s_sib[i])
        later = (chip.astype(F32) + early.astype(F32)).astype(BF16)
        s_mine[c, i] = jnp.where(c == 0, chip, later)
        s_other[i] = jnp.where(c == 0, later, chip)
        p_step[i] = jnp.where(c == 0, mine[1], other[1]).astype(F32) + dot(
            chip, jnp.where(c == 0, mine[0], other[0]), 1, 0
        )
    s_swap = remote(s_other, s_mine.at[c], core_send.at[2], core_recv.at[2], sibling)
    start(s_swap)
    s_swap_in = remote(s_other, s_mine.at[1 - c], core_send.at[2], core_recv.at[2], sibling)
    s_swap_in.wait_recv()

    for h in range(heads):
        s_h = s_mine[h // pair, h % pair]
        for j in range(2):
            qc, vc = chunk(q, h, j), chunk(v, h, j)
            f = (chunk(f_loc, h, j) + dot(qc, s_h, 1, 0)).astype(BF16)
            mixing = jnp.where(col <= row, dot(qc, f, 1, 1), 0.0).astype(BF16)
            o_part[j * CHUNK : (j + 1) * CHUNK, h * DH : (h + 1) * DH] = dot(mixing, vc, 1, 0)
            if j == 0:
                p_first[h] = dot(f, vc, 0, 0)

    wait_back(1)
    for i in range(pair):
        chip = p_pre[i]
        later = (chip.astype(F32) + p_step[i]).astype(BF16)
        p_mine[c, i] = jnp.where(c == 0, chip, later)
        p_other[i] = jnp.where(c == 0, later, chip)
    p_swap = remote(p_other, p_mine.at[c], core_send.at[3], core_recv.at[3], sibling)
    start(p_swap)
    p_swap_in = remote(p_other, p_mine.at[1 - c], core_send.at[3], core_recv.at[3], sibling)
    p_swap_in.wait_recv()
    for h in range(heads):
        p_h = p_mine[h // pair, h % pair]
        p_fin[0, h] = p_h
        p_fin[1, h] = (p_h.astype(F32) + p_first[h]).astype(BF16)

    rows_x = tokens // nx
    loads[4].wait()

    def n_copy(d, slot):
        return remote(n_out.at[d], n_in.at[slot], n_send.at[d], n_recv.at[slot], {"head": modx(d)})

    for d in (2, 1, 3, 0):
        target = modx(d)
        rows = pl.ds(pl.multiple_of(target * rows_x, rows_x), rows_x)
        part = target // (CHUNK // rows_x)
        for h in range(heads):
            cols = slice(h * DH, (h + 1) * DH)
            attended = o_part[rows, cols] + dot(q[rows, cols], p_fin[part, h], 1, 0)
            mean_square = jnp.mean(attended * attended, axis=-1, keepdims=True)
            n_out[d, :, cols] = (attended * lax.rsqrt(mean_square + EPS) * gain[:, cols]).astype(BF16)
        if d:
            start(n_copy(d, x))
    relay_x((4, 5))
    relay_y((2, 3))

    loads[3].wait()
    tile = 512
    n_cols = out_ref.shape[1]

    def project(rows_in, quarter, first, last):
        for begin in range(0, n_cols, tile):
            cols = slice(begin, begin + tile)
            part = dot(rows_in, w[quarter, :, cols], 1, 0)
            if not first:
                part = part + acc[:, cols]
            if last:
                out_ref[:, cols] = part.astype(BF16)
            else:
                acc[:, cols] = part

    project(n_out[0], x, True, False)
    relay_y((4, 5))
    for offset in (-1, 1, 2):
        quarter = modx(offset)
        for number, (of, half) in enumerate(X_PIECES):
            if of == offset:
                core_copy(number, 1 - c).wait_recv()
                core_y_copy(number, 1 - c).wait_recv()
        n_copy(offset % nx, quarter).wait_recv()
        project(n_in[quarter], quarter, False, offset == 2)

    for wait in pending:
        wait()
    drain_in(0)
    drain_in(1)

    @pl.when(is_worker)
    def _():
        for kind in range(2):
            for d in range(1, nz):
                back_copy(kind, my_head, d).wait_send()
            for d in range(1, ny):
                total_copy(kind, d, y).wait_send()


def shards(ny, nz, nx, queries, key_vectors, value_vectors, norm_gain, out_weight):
    tokens, width = queries.shape
    heads = width // DH
    pair = heads // 2
    depth, n_cols = out_weight.shape

    def matrices(*lead, kind=BF16):
        return pltpu.VMEM(lead + (DH, DH), kind)

    return pl.pallas_call(
        functools.partial(kernel, ny, nz, nx),
        out_shape=jax.ShapeDtypeStruct((tokens // nx, n_cols), BF16),
        in_specs=[pl.BlockSpec(memory_space=pltpu.HBM)] * 5,
        out_specs=pl.BlockSpec(memory_space=pltpu.VMEM),
        scratch_shapes=[
            pltpu.VMEM((tokens, width), BF16),
            pltpu.VMEM((tokens, width), BF16),
            pltpu.VMEM((tokens, width), BF16),
            pltpu.VMEM((nx, depth, n_cols), BF16),
            pltpu.VMEM((1, width), F32),
            matrices(heads),
            matrices(2, pair),
            matrices(2, pair, 2),
            matrices(pair),
            matrices(pair, 2),
            matrices(pair),
            matrices(pair, 2),
            matrices(nz),
            matrices(nz, 2),
            matrices(nz, kind=F32),
            matrices(nz),
            matrices(nz),
            matrices(2),
            matrices(2, ny),
            matrices(pair),
            matrices(pair),
            matrices(pair, kind=F32),
            matrices(pair),
            matrices(pair),
            matrices(2, pair),
            matrices(2, pair),
            pltpu.VMEM((tokens, width), F32),
            matrices(heads, kind=F32),
            pltpu.VMEM((tokens, width), F32),
            matrices(2, heads),
            pltpu.VMEM((nx, tokens // nx, width), BF16),
            pltpu.VMEM((nx, tokens // nx, width), BF16),
            pltpu.VMEM((tokens // nx, n_cols), F32),
            pltpu.SemaphoreType.DMA((5,)),
            pltpu.SemaphoreType.DMA((4,)),
            pltpu.SemaphoreType.DMA((4,)),
            pltpu.SemaphoreType.DMA((2, pair)),
            pltpu.SemaphoreType.DMA((2, nz)),
            pltpu.SemaphoreType.DMA((2, nz)),
            pltpu.SemaphoreType.DMA((2, pair)),
            pltpu.SemaphoreType.DMA((2, ny)),
            pltpu.SemaphoreType.DMA((2, ny)),
            pltpu.SemaphoreType.DMA((nx,)),
            pltpu.SemaphoreType.DMA((nx,)),
            pltpu.SemaphoreType.DMA((24,)),
            pltpu.SemaphoreType.DMA((24,)),
        ],
        compiler_params=pltpu.CompilerParams(
            collective_id=0, has_side_effects=True, vmem_limit_bytes=63 * 1024 * 1024
        ),
    )(queries, key_vectors, value_vectors, norm_gain.reshape(1, width), out_weight)


def solution(mesh):
    seq, nx = mesh.shape["seq"], mesh.shape["head"]
    ny = 4 if seq == 64 else 2
    nz = seq // (2 * ny)
    split = Mesh(mesh.devices.reshape(ny, nz, 2, nx), SEQ_HEAD)
    in_specs = (P(SEQ, "head"), P(SEQ, "head"), P(SEQ, "head"), P("head"), P("head", None))
    out_specs = P(SEQ_HEAD, None)
    return jax.shard_map(
        functools.partial(shards, ny, nz, nx), mesh=split, in_specs=in_specs, out_specs=out_specs, check_vma=False
    )
```

time: 61.9 us -> 48.9 us (0.79); the launches traced: 60.8 us -> 48.8 us
  Pallas kernels: 54.6 us -> 46.9 us
  local copies, waits for them, and re-layouts: 6.19 us -> 1.88 us
    pallas_call x1, Pallas kernels: 54.6 us -> 46.9 us  [shards(): pl.pallas_call(functools.partial(kernel, ny, nz, nx), out_shape=jax.Shape...]
    unnamed x11 -> x1, local copies, waits for them, and re-layouts: 6.19 us -> 1.88 us
where the time goes in v2:
time: 48.9 us; the launch traced here: 48.8 us
  Pallas kernels  46.9 us (96%)
  local copies, waits for them, and re-layouts  1.88 us (4%)
    pallas_call x1, Pallas kernels, shards(): pl.pallas_call(functools.partial(kernel, ny, nz, nx), out_shape=jax.Shape...  46.9 us
    unnamed x1, local copies, waits for them, and re-layouts  1.88 us

profile of v2, /device:TPU:1, one launch (start us, length us, event | category | flops | bytes accessed | tf_op | source)
XLA Modules:
  0.0 48.8 jit_solution(8150081522831943065)
XLA Ops:
  0.0 46.9 %shard_map.55 = bf16[128,2048]{1,0:T(8,128)(2,1)} custom-call(bf16[512,512]{1,0:T(8,128)(2,1)} %q_hbm.1, bf16[512,512]{1,0:T(8,128)(2,1)} %k_hbm.1, bf16[512,512]{1,0:T(8,128)(2,1)} %v_hbm.1, f32[1,512]{1,0:T(1,128)} %bitcast.1, bf16[512,2048]{1,0:T(8,128)(2,1)} %w_hbm.1), custom_call_target="tpu_custom_call" | custom-call | tf_op jit(solution)/shard_map/pallas_call | solution.py:440
  46.9 1.9 %copy.7 = bf16[128,2048]{1,0:T(8,128)(2,1)} copy(bf16[128,2048]{1,0:T(8,128)(2,1)} %shard_map.55) | data formatting | bytes 1048576

commit v3 on v2

--- a/solution.py
+++ b/solution.py
@@ -60,6 +60,7 @@
     p_other,
     s_mine,
     p_mine,
+    v_t,
     f_loc,
     p_first,
     o_part,
@@ -186,8 +187,9 @@
 
     def send_total(kind, total):
         y_out[kind] = total.astype(BF16)
-        for d in range(1, ny):
-            total_copy(kind, d, y).start()
+        for d in (2, 1, 3):
+            if d < ny:
+                total_copy(kind, d, y).start()
 
     def wait_totals(kind):
         base = jnp.zeros((DH, DH), F32)
@@ -257,18 +259,21 @@
         s_loc[h // pair, h % pair] = (first + dot(chunk(k, h, 1), chunk(k, h, 1), 0, 0)).astype(BF16)
     loads[1].wait()
     loads[2].wait()
+    strict, causal = col < row, col <= row
+    blocks = [(h, j) for h in range(heads) for j in range(2)]
     for h in range(heads):
-        pairs = jnp.zeros((DH, DH), F32)
-        cross = jnp.zeros((DH, DH), F32)
-        for j in range(2):
-            qc, kc, vc = chunk(q, h, j), chunk(k, h, j), chunk(v, h, j)
-            scores = jnp.where(col < row, dot(qc, kc, 1, 1), 0.0).astype(BF16)
-            f = dot(scores, kc, 1, 0)
-            if j == 1:
-                f = f + dot(qc, s_first[h], 1, 0)
-            f_loc[j * CHUNK : (j + 1) * CHUNK, h * DH : (h + 1) * DH] = f
-            pairs = pairs + dot(f.astype(BF16), vc, 0, 0)
-            cross = cross + dot(qc, vc, 0, 0)
+        v_t[h] = v[:, h * DH : (h + 1) * DH].T
+    scores = [jnp.where(strict, dot(chunk(q, h, j), chunk(k, h, j), 1, 1), 0.0).astype(BF16) for h, j in blocks]
+    fs = []
+    for n, (h, j) in enumerate(blocks):
+        f = dot(scores[n], chunk(k, h, j), 1, 0)
+        if j == 1:
+            f = f + dot(chunk(q, h, j), s_first[h], 1, 0)
+        f_loc[j * CHUNK : (j + 1) * CHUNK, h * DH : (h + 1) * DH] = f
+        fs.append(f.astype(BF16))
+    for h in range(heads):
+        cross = dot(v_t[h], q[:, h * DH : (h + 1) * DH], 1, 0)
+        pairs = dot(v_t[h, :, :CHUNK], fs[2 * h], 1, 0) + dot(v_t[h, :, CHUNK:], fs[2 * h + 1], 1, 0)
         cp_loc[h // pair, h % pair, 0] = cross.astype(BF16)
         cp_loc[h // pair, h % pair, 1] = pairs.astype(BF16)
 
@@ -290,7 +295,7 @@
         early = jnp.where(c == 0, s_loc[c, i], s_sib[i])
         late = jnp.where(c == 0, other[0], mine[0])
         cp_chip[i, 0] = (mine[0].astype(F32) + other[0].astype(F32)).astype(BF16)
-        cp_chip[i, 1] = (mine[1].astype(F32) + other[1].astype(F32) + dot(early, late, 1, 0)).astype(BF16)
+        cp_chip[i, 1] = (mine[1].astype(F32) + other[1].astype(F32) + dot(late, early, 1, 0)).astype(BF16)
     send_in(1)
 
     @pl.when(is_worker)
@@ -314,7 +319,7 @@
         total = jnp.zeros((DH, DH), F32)
         for r in range(nz):
             running[r] = total
-            total = total + cp_arr[r, 1].astype(F32) + dot(s_back[r], cp_arr[r, 0], 1, 0)
+            total = total + cp_arr[r, 1].astype(F32) + dot(cp_arr[r, 0], s_back[r], 1, 0)
         send_total(1, total)
 
     relay_x((2, 3))
@@ -336,22 +341,26 @@
         s_mine[c, i] = jnp.where(c == 0, chip, later)
         s_other[i] = jnp.where(c == 0, later, chip)
         p_step[i] = jnp.where(c == 0, mine[1], other[1]).astype(F32) + dot(
-            chip, jnp.where(c == 0, mine[0], other[0]), 1, 0
+            jnp.where(c == 0, mine[0], other[0]), chip, 1, 0
         )
     s_swap = remote(s_other, s_mine.at[c], core_send.at[2], core_recv.at[2], sibling)
     start(s_swap)
+    relay_x((4, 5))
     s_swap_in = remote(s_other, s_mine.at[1 - c], core_send.at[2], core_recv.at[2], sibling)
     s_swap_in.wait_recv()
 
+    fs = []
+    for h, j in blocks:
+        f = chunk(f_loc, h, j) + dot(chunk(q, h, j), s_mine[h // pair, h % pair], 1, 0)
+        fs.append(f.astype(BF16))
+    mixing = [
+        jnp.where(causal, dot(chunk(q, h, j), fs[n], 1, 1), 0.0).astype(BF16) for n, (h, j) in enumerate(blocks)
+    ]
+    for n, (h, j) in enumerate(blocks):
+        o_part[j * CHUNK : (j + 1) * CHUNK, h * DH : (h + 1) * DH] = dot(mixing[n], chunk(v, h, j), 1, 0)
     for h in range(heads):
-        s_h = s_mine[h // pair, h % pair]
-        for j in range(2):
-            qc, vc = chunk(q, h, j), chunk(v, h, j)
-            f = (chunk(f_loc, h, j) + dot(qc, s_h, 1, 0)).astype(BF16)
-            mixing = jnp.where(col <= row, dot(qc, f, 1, 1), 0.0).astype(BF16)
-            o_part[j * CHUNK : (j + 1) * CHUNK, h * DH : (h + 1) * DH] = dot(mixing, vc, 1, 0)
-            if j == 0:
-                p_first[h] = dot(f, vc, 0, 0)
+        p_first[h // pair, h % pair] = dot(v_t[h, :, :CHUNK], fs[2 * h], 1, 0)
+    relay_y((2, 3))
 
     wait_back(1)
     for i in range(pair):
@@ -362,40 +371,46 @@
     p_swap = remote(p_other, p_mine.at[c], core_send.at[3], core_recv.at[3], sibling)
     start(p_swap)
     p_swap_in = remote(p_other, p_mine.at[1 - c], core_send.at[3], core_recv.at[3], sibling)
-    p_swap_in.wait_recv()
-    for h in range(heads):
-        p_h = p_mine[h // pair, h % pair]
-        p_fin[0, h] = p_h
-        p_fin[1, h] = (p_h.astype(F32) + p_first[h]).astype(BF16)
 
     rows_x = tokens // nx
     loads[4].wait()
 
-    def n_copy(d, slot):
-        return remote(n_out.at[d], n_in.at[slot], n_send.at[d], n_recv.at[slot], {"head": modx(d)})
-
-    for d in (2, 1, 3, 0):
-        target = modx(d)
-        rows = pl.ds(pl.multiple_of(target * rows_x, rows_x), rows_x)
-        part = target // (CHUNK // rows_x)
-        for h in range(heads):
-            cols = slice(h * DH, (h + 1) * DH)
-            attended = o_part[rows, cols] + dot(q[rows, cols], p_fin[part, h], 1, 0)
-            mean_square = jnp.mean(attended * attended, axis=-1, keepdims=True)
-            n_out[d, :, cols] = (attended * lax.rsqrt(mean_square + EPS) * gain[:, cols]).astype(BF16)
-        if d:
-            start(n_copy(d, x))
-    relay_x((4, 5))
-    relay_y((2, 3))
+    def n_copy(d, g, slot):
+        return remote(n_out.at[d, g], n_in.at[slot, g], n_send.at[d, g], n_recv.at[slot, g], {"head": modx(d)})
+
+    for step in range(2):
+        g = c if step == 0 else 1 - c
+        if step == 1:
+            p_swap_in.wait_recv()
+        for i in range(pair):
+            p_h = p_mine[g, i]
+            p_fin[0, i] = p_h
+            p_fin[1, i] = (p_h.astype(F32) + p_first[g, i]).astype(BF16)
+        for d in (2, 1, 3, 0):
+            target = modx(d)
+            rows = pl.ds(pl.multiple_of(target * rows_x, rows_x), rows_x)
+            part = target // (CHUNK // rows_x)
+            for i in range(pair):
+                cols = pl.ds(pl.multiple_of(g * (pair * DH) + i * DH, DH), DH)
+                attended = o_part[rows, cols] + dot(q[rows, cols], p_fin[part, i], 1, 1)
+                mean_square = jnp.mean(attended * attended, axis=-1, keepdims=True)
+                n_out[d, g, :, i * DH : (i + 1) * DH] = (
+                    attended * lax.rsqrt(mean_square + EPS) * gain[:, cols]
+                ).astype(BF16)
+            if d:
+                start(n_copy(d, g, x))
 
     loads[3].wait()
     tile = 512
     n_cols = out_ref.shape[1]
 
-    def project(rows_in, quarter, first, last):
+    half = w.shape[1] // 2
+
+    def project(rows_in, slot, quarter, first, last):
         for begin in range(0, n_cols, tile):
             cols = slice(begin, begin + tile)
-            part = dot(rows_in, w[quarter, :, cols], 1, 0)
+            part = dot(rows_in[slot, 0], w[quarter, :half, cols], 1, 0)
+            part = part + dot(rows_in[slot, 1], w[quarter, half:, cols], 1, 0)
             if not first:
                 part = part + acc[:, cols]
             if last:
@@ -403,16 +418,17 @@
             else:
                 acc[:, cols] = part
 
-    project(n_out[0], x, True, False)
+    project(n_out, 0, x, True, False)
     relay_y((4, 5))
     for offset in (-1, 1, 2):
         quarter = modx(offset)
-        for number, (of, half) in enumerate(X_PIECES):
+        for number, (of, _) in enumerate(X_PIECES):
             if of == offset:
                 core_copy(number, 1 - c).wait_recv()
                 core_y_copy(number, 1 - c).wait_recv()
-        n_copy(offset % nx, quarter).wait_recv()
-        project(n_in[quarter], quarter, False, offset == 2)
+        for g in range(2):
+            n_copy(offset % nx, g, quarter).wait_recv()
+        project(n_in, quarter, quarter, False, offset == 2)
 
     for wait in pending:
         wait()
@@ -437,6 +453,7 @@
     def matrices(*lead, kind=BF16):
         return pltpu.VMEM(lead + (DH, DH), kind)
 
+    operands = (queries, key_vectors, value_vectors, norm_gain.reshape(1, width), out_weight)
     return pl.pallas_call(
         functools.partial(kernel, ny, nz, nx),
         out_shape=jax.ShapeDtypeStruct((tokens // nx, n_cols), BF16),
@@ -469,12 +486,13 @@
             matrices(pair),
             matrices(2, pair),
             matrices(2, pair),
+            pltpu.VMEM((heads, DH, tokens), BF16),
             pltpu.VMEM((tokens, width), F32),
-            matrices(heads, kind=F32),
+            matrices(2, pair, kind=F32),
             pltpu.VMEM((tokens, width), F32),
-            matrices(2, heads),
-            pltpu.VMEM((nx, tokens // nx, width), BF16),
-            pltpu.VMEM((nx, tokens // nx, width), BF16),
+            matrices(2, pair),
+            pltpu.VMEM((nx, 2, tokens // nx, width // 2), BF16),
+            pltpu.VMEM((nx, 2, tokens // nx, width // 2), BF16),
             pltpu.VMEM((tokens // nx, n_cols), F32),
             pltpu.SemaphoreType.DMA((5,)),
             pltpu.SemaphoreType.DMA((4,)),
@@ -485,15 +503,15 @@
             pltpu.SemaphoreType.DMA((2, pair)),
             pltpu.SemaphoreType.DMA((2, ny)),
             pltpu.SemaphoreType.DMA((2, ny)),
-            pltpu.SemaphoreType.DMA((nx,)),
-            pltpu.SemaphoreType.DMA((nx,)),
+            pltpu.SemaphoreType.DMA((nx, 2)),
+            pltpu.SemaphoreType.DMA((nx, 2)),
             pltpu.SemaphoreType.DMA((24,)),
             pltpu.SemaphoreType.DMA((24,)),
         ],
         compiler_params=pltpu.CompilerParams(
-            collective_id=0, has_side_effects=True, vmem_limit_bytes=63 * 1024 * 1024
+            collective_id=0, has_side_effects=True, vmem_limit_bytes=48 * 1024 * 1024
         ),
-    )(queries, key_vectors, value_vectors, norm_gain.reshape(1, width), out_weight)
+    )(*[pltpu.with_memory_space_constraint(array, pltpu.HBM) for array in operands])
 
 
 def solution(mesh):

time: 48.9 us -> 45.5 us (0.930)
  Pallas kernels: 46.9 us -> 44.7 us
  local copies, waits for them, and re-layouts: 1.88 us -> 0.8 us
    pallas_call x1, Pallas kernels: 46.9 us -> 44.7 us  [shards(): pl.pallas_call(functools.partial(kernel, ny, nz, nx), out_shape=jax.Shape...]
    unnamed x1, local copies, waits for them, and re-layouts: 1.88 us -> 0.8 us
where the time goes in v3:
time: 45.5 us
  Pallas kernels  44.7 us (98%)
  local copies, waits for them, and re-layouts  0.8 us (2%)
    pallas_call x1, Pallas kernels, shards(): pl.pallas_call(functools.partial(kernel, ny, nz, nx), out_shape=jax.Shape...  44.7 us

profile of v3, /device:TPU:1, one launch (start us, length us, event | category | flops | bytes accessed | tf_op | source)
XLA Modules:
  0.0 45.5 jit_solution(17908791204195506581)
XLA Ops:
  0.0 44.7 %shard_map.55 = bf16[128,2048]{1,0:T(8,128)(2,1)S(1)} custom-call(bf16[512,512]{1,0:T(8,128)(2,1)} %q_hbm.1, bf16[512,512]{1,0:T(8,128)(2,1)} %k_hbm.1, bf16[512,512]{1,0:T(8,128)(2,1)} %v_hbm.1, f32[1,512]{1,0:T(1,128)} %bitcast.1, bf16[512,2048]{1,0:T(8,128)(2,1)} %w_hbm.1), custom_call_target="tpu_custom_call" | custom-call | tf_op jit(solution)/shard_map/pallas_call | solution.py:457
  44.7 0.8 %copy.7 = bf16[128,2048]{1,0:T(8,128)(2,1)} copy(bf16[128,2048]{1,0:T(8,128)(2,1)S(1)} %shard_map.55) | data formatting | bytes 1048576

commit v4 on v3

--- a/solution.py
+++ b/solution.py
@@ -48,7 +48,9 @@
     cp_chip,
     s_arr,
     cp_arr,
-    running,
+    s_run,
+    p_run,
+    c_run,
     s_back,
     p_back,
     y_out,
@@ -112,11 +114,26 @@
         copy.start()
         pending.append(copy.wait_send)
 
+    spacing = nz // heads
+    is_worker = (lax.rem(z, spacing) == 0) & (z // (spacing * pair) == c)
+    my_head = lax.rem(z // spacing, pair)
+
     barrier = pltpu.get_barrier_semaphore()
-    greeted = [{"seq_1": modz(d)} for d in range(1, nz)] + [{"seq_2": 1 - c}]
-    greeted += [{"seq_0": mody(d)} for d in range(1, ny)] + [{"head": modx(d)} for d in range(1, nx)]
-    for peer in greeted:
+
+    def greet(peer):
         pl.semaphore_signal(barrier, inc=1, device_id=peer, device_id_type=pl.DeviceIdType.MESH)
+
+    for d in range(1, ny):
+        greet({"seq_0": mody(d)})
+    for d in range(1, nx):
+        greet({"head": modx(d)})
+    greet({"seq_2": 1 - c})
+
+    @pl.when(is_worker)
+    def _():
+        for d in FAR_FIRST:
+            if d < nz:
+                greet({"seq_1": modz(d)})
 
     loads = [
         pltpu.make_async_copy(src, dst, load_sem.at[i])
@@ -128,10 +145,6 @@
     def chunk(ref, h, j):
         return ref[j * CHUNK : (j + 1) * CHUNK, h * DH : (h + 1) * DH]
 
-    spacing = nz // heads
-    is_worker = (lax.rem(z, spacing) == 0) & (z // (spacing * pair) == c)
-    my_head = lax.rem(z // spacing, pair)
-
     def worker_z(i):
         return (c * pair + i) * spacing
 
@@ -139,8 +152,15 @@
         src, dst = ((s_chip, s_arr), (cp_chip, cp_arr))[kind]
         return remote(src.at[i], dst.at[slot], in_send.at[kind, i], in_recv.at[kind, slot], device_id)
 
+    def distance(i):
+        ahead = lax.rem(worker_z(i) - z + nz, nz)
+        return jnp.minimum(ahead, nz - ahead)
+
+    farther = jnp.where(distance(0) < distance(pair - 1), pair - 1, 0)
+
     def send_in(kind):
-        for i in range(pair):
+        for n in range(pair):
+            i = lax.rem(farther + n, pair)
             here = z == worker_z(i)
             copy = in_copy(kind, i, z, {"seq_1": worker_z(i)})
 
@@ -181,22 +201,24 @@
                 back_copy(kind, i, 1).wait_recv()
 
     def total_copy(kind, d, slot):
+        part = (pl.ds(0, 1), pl.ds(1, 2))[kind]
         return remote(
-            y_out.at[kind], y_in.at[kind, slot], y_send.at[kind, d], y_recv.at[kind, slot], {"seq_0": mody(d)}
+            y_out.at[part], y_in.at[slot, part], y_send.at[kind, d], y_recv.at[kind, slot], {"seq_0": mody(d)}
         )
 
-    def send_total(kind, total):
-        y_out[kind] = total.astype(BF16)
+    def send_totals(kind):
         for d in (2, 1, 3):
             if d < ny:
                 total_copy(kind, d, y).start()
 
     def wait_totals(kind):
+        for d in range(1, ny):
+            total_copy(kind, d, mody(d)).wait_recv()
+
+    def s_base_until(limit):
         base = jnp.zeros((DH, DH), F32)
-        for d in range(1, ny):
-            other = mody(d)
-            total_copy(kind, d, other).wait_recv()
-            base = base + jnp.where(other < y, y_in[kind, other].astype(F32), 0.0)
+        for r in range(ny - 1):
+            base = base + jnp.where(r < limit, y_in[r, 0].astype(F32), 0.0)
         return base
 
     colour = lax.rem(y, 2)
@@ -277,7 +299,7 @@
         cp_loc[h // pair, h % pair, 0] = cross.astype(BF16)
         cp_loc[h // pair, h % pair, 1] = pairs.astype(BF16)
 
-    pl.semaphore_wait(barrier, len(greeted))
+    pl.semaphore_wait(barrier, nx - 1 + ny - 1 + 1 + pair - is_worker.astype(jnp.int32))
     sibling = {"seq_2": 1 - c}
     s_core = remote(s_loc.at[1 - c], s_sib, core_send.at[0], core_recv.at[0], sibling)
     cp_core = remote(cp_loc.at[1 - c], cp_sib, core_send.at[1], core_recv.at[1], sibling)
@@ -303,34 +325,49 @@
         wait_in(0)
         total = jnp.zeros((DH, DH), F32)
         for r in range(nz):
-            running[r] = total
+            s_run[r] = total
             total = total + s_arr[r].astype(F32)
-        send_total(0, total)
+        y_out[0] = total.astype(BF16)
+        send_totals(0)
+        y_in[y, 0] = total.astype(BF16)
 
     relay_x((0, 1))
 
     @pl.when(is_worker)
     def _():
-        base = wait_totals(0)
+        wait_in(1)
+        pairs = jnp.zeros((DH, DH), F32)
+        cross = jnp.zeros((DH, DH), F32)
         for r in range(nz):
-            s_back[r] = (running[r] + base).astype(BF16)
+            p_run[r] = pairs
+            c_run[r] = cross.astype(BF16)
+            pairs = pairs + (cp_arr[r, 1].astype(F32) + dot(cp_arr[r, 0], s_run[r].astype(BF16), 1, 0))
+            cross = cross + cp_arr[r, 0].astype(F32)
+        y_out[1] = cross.astype(BF16)
+        y_out[2] = pairs.astype(BF16)
+        send_totals(1)
+        y_in[y, 1] = cross.astype(BF16)
+        y_in[y, 2] = pairs.astype(BF16)
+        wait_totals(0)
+        s_base = s_base_until(y)
+        for r in range(nz):
+            s_back[r] = (s_run[r] + s_base).astype(BF16)
         send_back(0)
-        wait_in(1)
-        total = jnp.zeros((DH, DH), F32)
+        s_base = s_base.astype(BF16)
         for r in range(nz):
-            running[r] = total
-            total = total + cp_arr[r, 1].astype(F32) + dot(cp_arr[r, 0], s_back[r], 1, 0)
-        send_total(1, total)
+            p_run[r] = p_run[r] + dot(c_run[r], s_base, 1, 0)
+        before = [s_base_until(r).astype(BF16) for r in range(ny - 1)]
+        wait_totals(1)
+        p_base = jnp.zeros((DH, DH), F32)
+        for r in range(ny - 1):
+            line = y_in[r, 2].astype(F32) + dot(y_in[r, 1], before[r], 1, 0)
+            p_base = p_base + jnp.where(r < y, line, 0.0)
+        for r in range(nz):
+            p_back[r] = (p_run[r] + p_base).astype(BF16)
+        send_back(1)
 
     relay_x((2, 3))
     relay_y((0, 1))
-
-    @pl.when(is_worker)
-    def _():
-        base = wait_totals(1)
-        for r in range(nz):
-            p_back[r] = (running[r] + base).astype(BF16)
-        send_back(1)
 
     wait_back(0)
     for i in range(pair):
@@ -475,10 +512,12 @@
             matrices(nz),
             matrices(nz, 2),
             matrices(nz, kind=F32),
+            matrices(nz, kind=F32),
             matrices(nz),
             matrices(nz),
-            matrices(2),
-            matrices(2, ny),
+            matrices(nz),
+            matrices(3),
+            matrices(ny, 3),
             matrices(pair),
             matrices(pair),
             matrices(pair, kind=F32),

time: 45.5 us -> 47.9 us (1.053)
  Pallas kernels: 44.7 us -> 47 us
    pallas_call x1, Pallas kernels: 44.7 us -> 47 us  [shards(): pl.pallas_call(functools.partial(kernel, ny, nz, nx), out_shape=jax.Shape...]
where the time goes in v4:
time: 47.9 us; the launch traced here: 47.8 us
  Pallas kernels  47 us (98%)
  local copies, waits for them, and re-layouts  0.8 us (2%)
    pallas_call x1, Pallas kernels, shards(): pl.pallas_call(functools.partial(kernel, ny, nz, nx), out_shape=jax.Shape...  47 us

profile of v4, /device:TPU:1, one launch (start us, length us, event | category | flops | bytes accessed | tf_op | source)
XLA Modules:
  0.0 47.8 jit_solution(13243231810711750228)
XLA Ops:
  0.0 47.0 %shard_map.55 = bf16[128,2048]{1,0:T(8,128)(2,1)S(1)} custom-call(bf16[512,512]{1,0:T(8,128)(2,1)} %q_hbm.1, bf16[512,512]{1,0:T(8,128)(2,1)} %k_hbm.1, bf16[512,512]{1,0:T(8,128)(2,1)} %v_hbm.1, f32[1,512]{1,0:T(1,128)} %bitcast.1, bf16[512,2048]{1,0:T(8,128)(2,1)} %w_hbm.1), custom_call_target="tpu_custom_call" | custom-call | tf_op jit(solution)/shard_map/pallas_call | solution.py:494
  47.0 0.8 %copy.7 = bf16[128,2048]{1,0:T(8,128)(2,1)} copy(bf16[128,2048]{1,0:T(8,128)(2,1)S(1)} %shard_map.55) | data formatting | bytes 1048576

commit v5 on v4

--- a/solution.py
+++ b/solution.py
@@ -221,16 +221,20 @@
             base = base + jnp.where(r < limit, y_in[r, 0].astype(F32), 0.0)
         return base
 
-    colour = lax.rem(y, 2)
+    colour = lax.rem(y + z, 2)
     piece_rows = w.shape[1] // 8
 
-    def rows_of(colour_of, core_of, half):
+    def rows_of(colour_of, core_of, half, part=None):
         first = colour_of * (4 * piece_rows) + core_of * (2 * piece_rows) + half * piece_rows
-        return pl.ds(pl.multiple_of(first, piece_rows), piece_rows)
-
-    def piece(i, colour_of, core_of):
+        count = piece_rows
+        if part is not None:
+            count = piece_rows // 2
+            first = first + part * count
+        return pl.ds(pl.multiple_of(first, count), count)
+
+    def piece(i, colour_of, core_of, part=None):
         offset, half = X_PIECES[i]
-        return w.at[modx(offset), rows_of(colour_of, core_of, half)]
+        return w.at[modx(offset), rows_of(colour_of, core_of, half, part)]
 
     def w_copy(number, src, dst, device_id):
         return remote(src, dst, w_send.at[number], w_recv.at[number], device_id)
@@ -251,26 +255,34 @@
         ref = piece(number, colour, core_of)
         return w_copy(6 + number, ref, ref, {"seq_2": 1 - c})
 
-    def y_copy(number, colour_of):
-        ref = piece(number, colour_of, c)
-        return w_copy(12 + number, ref, ref, {"seq_0": mody(1 if X_PIECES[number][1] == 0 else -1)})
-
-    def core_y_copy(number, core_of):
-        ref = piece(number, 1 - colour, core_of)
-        return w_copy(18 + number, ref, ref, {"seq_2": 1 - c})
+    def parts_of(number):
+        return (None,) if number < 4 else (0, 1)
+
+    def plane_copy(number, colour_of, part):
+        ref = piece(number, colour_of, c, part)
+        step = 1 if X_PIECES[number][1] == 0 else -1
+        if part == 1:
+            return w_copy(20 + number, ref, ref, {"seq_1": modz(step + nz)})
+        return w_copy(12 + number, ref, ref, {"seq_0": mody(step)})
+
+    def core_plane_copy(number, core_of, part):
+        ref = piece(number, 1 - colour, core_of, part)
+        return w_copy((22 if part == 1 else 18) + number, ref, ref, {"seq_2": 1 - c})
 
     def relay_x(numbers):
         for number in numbers:
             x_arrival(number).wait_recv()
             if number < 2:
                 start(x_send(4 + number))
-            start(y_copy(number, colour))
+            for part in parts_of(number):
+                start(plane_copy(number, colour, part))
             start(core_copy(number, c))
 
-    def relay_y(numbers):
+    def relay_plane(numbers):
         for number in numbers:
-            y_copy(number, 1 - colour).wait_recv()
-            start(core_y_copy(number, c))
+            for part in parts_of(number):
+                plane_copy(number, 1 - colour, part).wait_recv()
+                start(core_plane_copy(number, c, part))
 
     row = lax.broadcasted_iota(jnp.int32, (CHUNK, CHUNK), 0)
     col = lax.broadcasted_iota(jnp.int32, (CHUNK, CHUNK), 1)
@@ -356,6 +368,11 @@
         s_base = s_base.astype(BF16)
         for r in range(nz):
             p_run[r] = p_run[r] + dot(c_run[r], s_base, 1, 0)
+
+    relay_x((2, 3))
+
+    @pl.when(is_worker)
+    def _():
         before = [s_base_until(r).astype(BF16) for r in range(ny - 1)]
         wait_totals(1)
         p_base = jnp.zeros((DH, DH), F32)
@@ -366,8 +383,7 @@
             p_back[r] = (p_run[r] + p_base).astype(BF16)
         send_back(1)
 
-    relay_x((2, 3))
-    relay_y((0, 1))
+    relay_plane((0, 1))
 
     wait_back(0)
     for i in range(pair):
@@ -382,7 +398,6 @@
         )
     s_swap = remote(s_other, s_mine.at[c], core_send.at[2], core_recv.at[2], sibling)
     start(s_swap)
-    relay_x((4, 5))
     s_swap_in = remote(s_other, s_mine.at[1 - c], core_send.at[2], core_recv.at[2], sibling)
     s_swap_in.wait_recv()
 
@@ -397,7 +412,7 @@
         o_part[j * CHUNK : (j + 1) * CHUNK, h * DH : (h + 1) * DH] = dot(mixing[n], chunk(v, h, j), 1, 0)
     for h in range(heads):
         p_first[h // pair, h % pair] = dot(v_t[h, :, :CHUNK], fs[2 * h], 1, 0)
-    relay_y((2, 3))
+    relay_x((4, 5))
 
     wait_back(1)
     for i in range(pair):
@@ -437,6 +452,8 @@
             if d:
                 start(n_copy(d, g, x))
 
+    relay_plane((2, 3))
+
     loads[3].wait()
     tile = 512
     n_cols = out_ref.shape[1]
@@ -456,13 +473,14 @@
                 acc[:, cols] = part
 
     project(n_out, 0, x, True, False)
-    relay_y((4, 5))
+    relay_plane((4, 5))
     for offset in (-1, 1, 2):
         quarter = modx(offset)
         for number, (of, _) in enumerate(X_PIECES):
             if of == offset:
                 core_copy(number, 1 - c).wait_recv()
-                core_y_copy(number, 1 - c).wait_recv()
+                for part in parts_of(number):
+                    core_plane_copy(number, 1 - c, part).wait_recv()
         for g in range(2):
             n_copy(offset % nx, g, quarter).wait_recv()
         project(n_in, quarter, quarter, False, offset == 2)
@@ -544,8 +562,8 @@
             pltpu.SemaphoreType.DMA((2, ny)),
             pltpu.SemaphoreType.DMA((nx, 2)),
             pltpu.SemaphoreType.DMA((nx, 2)),
-            pltpu.SemaphoreType.DMA((24,)),
-            pltpu.SemaphoreType.DMA((24,)),
+            pltpu.SemaphoreType.DMA((28,)),
+            pltpu.SemaphoreType.DMA((28,)),
         ],
         compiler_params=pltpu.CompilerParams(
             collective_id=0, has_side_effects=True, vmem_limit_bytes=48 * 1024 * 1024

time: 47.9 us -> 44.9 us (0.937)
  Pallas kernels: 47 us -> 44.1 us
    pallas_call x1, Pallas kernels: 47 us -> 44.1 us  [shards(): pl.pallas_call(functools.partial(kernel, ny, nz, nx), out_shape=jax.Shape...]
where the time goes in v5:
time: 44.9 us
  Pallas kernels  44.1 us (98%)
  local copies, waits for them, and re-layouts  0.8 us (2%)
    pallas_call x1, Pallas kernels, shards(): pl.pallas_call(functools.partial(kernel, ny, nz, nx), out_shape=jax.Shape...  44.1 us

profile of v5, /device:TPU:1, one launch (start us, length us, event | category | flops | bytes accessed | tf_op | source)
XLA Modules:
  0.0 44.9 jit_solution(13968577053117013980)
XLA Ops:
  0.0 44.1 %shard_map.55 = bf16[128,2048]{1,0:T(8,128)(2,1)S(1)} custom-call(bf16[512,512]{1,0:T(8,128)(2,1)} %q_hbm.1, bf16[512,512]{1,0:T(8,128)(2,1)} %k_hbm.1, bf16[512,512]{1,0:T(8,128)(2,1)} %v_hbm.1, f32[1,512]{1,0:T(1,128)} %bitcast.1, bf16[512,2048]{1,0:T(8,128)(2,1)} %w_hbm.1), custom_call_target="tpu_custom_call" | custom-call | tf_op jit(solution)/shard_map/pallas_call | solution.py:512
  44.1 0.8 %copy.7 = bf16[128,2048]{1,0:T(8,128)(2,1)} copy(bf16[128,2048]{1,0:T(8,128)(2,1)S(1)} %shard_map.55) | data formatting | bytes 1048576

commit v6 on v5

--- a/solution.py
+++ b/solution.py
@@ -17,6 +17,7 @@
 EPS = 1e-06
 FAR_FIRST = (4, 3, 5, 2, 6, 1, 7)
 
+PARTS = ((0, 1), (0, 1), (None,), (None,), (0, 1), (0, 1))
 X_PIECES = ((-1, 0), (1, 1), (-1, 1), (1, 0), (2, 0), (2, 1))
 
 
@@ -239,50 +240,52 @@
     def w_copy(number, src, dst, device_id):
         return remote(src, dst, w_send.at[number], w_recv.at[number], device_id)
 
-    def x_send(number):
+    def unit(number, part):
+        return 2 * number + (part or 0)
+
+    def x_send(number, part):
         offset, half = X_PIECES[number]
         if number < 4:
-            rows = rows_of(colour, c, half)
-            return w_copy(number, w_hbm.at[rows], w.at[x, rows], {"head": modx(-offset)})
-        src = piece(number - 4, colour, c)
-        return w_copy(number, src, src, {"head": modx(1 if number == 4 else -1)})
-
-    def x_arrival(number):
-        ref = piece(number, colour, c)
-        return w_copy(number, ref, ref, {"head": modx(1)})
+            rows = rows_of(colour, c, half, part)
+            return w_copy(unit(number, part), w_hbm.at[rows], w.at[x, rows], {"head": modx(-offset)})
+        src = piece(number - 4, colour, c, part)
+        return w_copy(unit(number, part), src, src, {"head": modx(1 if number == 4 else -1)})
+
+    def x_arrival(number, part):
+        ref = piece(number, colour, c, part)
+        return w_copy(unit(number, part), ref, ref, {"head": modx(1)})
+
+    def plane_copy(number, part, colour_of):
+        ref = piece(number, colour_of, c, part)
+        step = 1 if X_PIECES[number][1] == 0 else -1
+        peer = {"seq_1": modz(step + nz)} if number >= 4 and part == 1 else {"seq_0": mody(step)}
+        return w_copy(12 + unit(number, part), ref, ref, peer)
 
     def core_copy(number, core_of):
         ref = piece(number, colour, core_of)
-        return w_copy(6 + number, ref, ref, {"seq_2": 1 - c})
-
-    def parts_of(number):
-        return (None,) if number < 4 else (0, 1)
-
-    def plane_copy(number, colour_of, part):
-        ref = piece(number, colour_of, c, part)
-        step = 1 if X_PIECES[number][1] == 0 else -1
-        if part == 1:
-            return w_copy(20 + number, ref, ref, {"seq_1": modz(step + nz)})
-        return w_copy(12 + number, ref, ref, {"seq_0": mody(step)})
-
-    def core_plane_copy(number, core_of, part):
+        return w_copy(24 + number, ref, ref, {"seq_2": 1 - c})
+
+    def core_plane_copy(number, part, core_of):
         ref = piece(number, 1 - colour, core_of, part)
-        return w_copy((22 if part == 1 else 18) + number, ref, ref, {"seq_2": 1 - c})
-
-    def relay_x(numbers):
-        for number in numbers:
-            x_arrival(number).wait_recv()
+        return w_copy(30 + unit(number, part), ref, ref, {"seq_2": 1 - c})
+
+    def relay_x(*units):
+        for number, part in units:
+            x_arrival(number, part).wait_recv()
             if number < 2:
-                start(x_send(4 + number))
-            for part in parts_of(number):
-                start(plane_copy(number, colour, part))
-            start(core_copy(number, c))
-
-    def relay_plane(numbers):
-        for number in numbers:
-            for part in parts_of(number):
-                plane_copy(number, 1 - colour, part).wait_recv()
-                start(core_plane_copy(number, c, part))
+                start(x_send(4 + number, part))
+            start(plane_copy(number, part, colour))
+        for number, part in units:
+            if part != 0:
+                start(core_copy(number, c))
+
+    def arrive_plane(number):
+        for part in PARTS[number]:
+            plane_copy(number, part, 1 - colour).wait_recv()
+            if number >= 4:
+                start(core_plane_copy(number, part, c))
+        if number < 4:
+            start(core_plane_copy(number, None, c))
 
     row = lax.broadcasted_iota(jnp.int32, (CHUNK, CHUNK), 0)
     col = lax.broadcasted_iota(jnp.int32, (CHUNK, CHUNK), 1)
@@ -317,8 +320,8 @@
     cp_core = remote(cp_loc.at[1 - c], cp_sib, core_send.at[1], core_recv.at[1], sibling)
     start(s_core)
     start(cp_core)
-    for number in range(4):
-        start(x_send(number))
+    for number, part in ((0, 0), (1, 0), (0, 1), (1, 1), (2, None), (3, None)):
+        start(x_send(number, part))
     s_core.wait_recv()
     for i in range(pair):
         s_chip[i] = (s_loc[c, i].astype(F32) + s_sib[i].astype(F32)).astype(BF16)
@@ -332,6 +335,8 @@
         cp_chip[i, 1] = (mine[1].astype(F32) + other[1].astype(F32) + dot(late, early, 1, 0)).astype(BF16)
     send_in(1)
 
+    relay_x((0, 0), (1, 0))
+
     @pl.when(is_worker)
     def _():
         wait_in(0)
@@ -343,7 +348,7 @@
         send_totals(0)
         y_in[y, 0] = total.astype(BF16)
 
-    relay_x((0, 1))
+    relay_x((0, 1), (1, 1))
 
     @pl.when(is_worker)
     def _():
@@ -368,11 +373,6 @@
         s_base = s_base.astype(BF16)
         for r in range(nz):
             p_run[r] = p_run[r] + dot(c_run[r], s_base, 1, 0)
-
-    relay_x((2, 3))
-
-    @pl.when(is_worker)
-    def _():
         before = [s_base_until(r).astype(BF16) for r in range(ny - 1)]
         wait_totals(1)
         p_base = jnp.zeros((DH, DH), F32)
@@ -382,8 +382,6 @@
         for r in range(nz):
             p_back[r] = (p_run[r] + p_base).astype(BF16)
         send_back(1)
-
-    relay_plane((0, 1))
 
     wait_back(0)
     for i in range(pair):
@@ -398,6 +396,9 @@
         )
     s_swap = remote(s_other, s_mine.at[c], core_send.at[2], core_recv.at[2], sibling)
     start(s_swap)
+    relay_x((2, None), (3, None))
+    arrive_plane(0)
+    arrive_plane(1)
     s_swap_in = remote(s_other, s_mine.at[1 - c], core_send.at[2], core_recv.at[2], sibling)
     s_swap_in.wait_recv()
 
@@ -412,7 +413,7 @@
         o_part[j * CHUNK : (j + 1) * CHUNK, h * DH : (h + 1) * DH] = dot(mixing[n], chunk(v, h, j), 1, 0)
     for h in range(heads):
         p_first[h // pair, h % pair] = dot(v_t[h, :, :CHUNK], fs[2 * h], 1, 0)
-    relay_x((4, 5))
+    relay_x((4, 0), (5, 0), (4, 1), (5, 1))
 
     wait_back(1)
     for i in range(pair):
@@ -452,7 +453,8 @@
             if d:
                 start(n_copy(d, g, x))
 
-    relay_plane((2, 3))
+    arrive_plane(2)
+    arrive_plane(3)
 
     loads[3].wait()
     tile = 512
@@ -473,14 +475,15 @@
                 acc[:, cols] = part
 
     project(n_out, 0, x, True, False)
-    relay_plane((4, 5))
+    arrive_plane(4)
+    arrive_plane(5)
     for offset in (-1, 1, 2):
         quarter = modx(offset)
         for number, (of, _) in enumerate(X_PIECES):
             if of == offset:
                 core_copy(number, 1 - c).wait_recv()
-                for part in parts_of(number):
-                    core_plane_copy(number, 1 - c, part).wait_recv()
+                for part in PARTS[number] if number >= 4 else (None,):
+                    core_plane_copy(number, part, 1 - c).wait_recv()
         for g in range(2):
             n_copy(offset % nx, g, quarter).wait_recv()
         project(n_in, quarter, quarter, False, offset == 2)
@@ -562,8 +565,8 @@
             pltpu.SemaphoreType.DMA((2, ny)),
             pltpu.SemaphoreType.DMA((nx, 2)),
             pltpu.SemaphoreType.DMA((nx, 2)),
-            pltpu.SemaphoreType.DMA((28,)),
-            pltpu.SemaphoreType.DMA((28,)),
+            pltpu.SemaphoreType.DMA((42,)),
+            pltpu.SemaphoreType.DMA((42,)),
         ],
         compiler_params=pltpu.CompilerParams(
             collective_id=0, has_side_effects=True, vmem_limit_bytes=48 * 1024 * 1024

time: 44.9 us -> 41.9 us (0.933)
  Pallas kernels: 44.1 us -> 41 us
    pallas_call x1, Pallas kernels: 44.1 us -> 41 us  [shards(): pl.pallas_call(functools.partial(kernel, ny, nz, nx), out_shape=jax.Shape...]
where the time goes in v6:
time: 41.9 us; the launch traced here: 41.8 us
  Pallas kernels  41 us (98%)
  local copies, waits for them, and re-layouts  0.8 us (2%)
    pallas_call x1, Pallas kernels, shards(): pl.pallas_call(functools.partial(kernel, ny, nz, nx), out_shape=jax.Shape...  41 us

profile of v6, /device:TPU:1, one launch (start us, length us, event | category | flops | bytes accessed | tf_op | source)
XLA Modules:
  0.0 41.8 jit_solution(6039601510462665858)
XLA Ops:
  0.0 41.0 %shard_map.55 = bf16[128,2048]{1,0:T(8,128)(2,1)S(1)} custom-call(bf16[512,512]{1,0:T(8,128)(2,1)} %q_hbm.1, bf16[512,512]{1,0:T(8,128)(2,1)} %k_hbm.1, bf16[512,512]{1,0:T(8,128)(2,1)} %v_hbm.1, f32[1,512]{1,0:T(1,128)} %bitcast.1, bf16[512,2048]{1,0:T(8,128)(2,1)} %w_hbm.1), custom_call_target="tpu_custom_call" | custom-call | tf_op jit(solution)/shard_map/pallas_call | solution.py:515
  41.0 0.8 %copy.7 = bf16[128,2048]{1,0:T(8,128)(2,1)} copy(bf16[128,2048]{1,0:T(8,128)(2,1)S(1)} %shard_map.55) | data formatting | bytes 1048576

commit v7 on v6

--- a/solution.py
+++ b/solution.py
@@ -140,7 +140,7 @@
         pltpu.make_async_copy(src, dst, load_sem.at[i])
         for i, (src, dst) in enumerate(((k_hbm, k), (q_hbm, q), (v_hbm, v), (w_hbm, w.at[x]), (gain_hbm, gain)))
     ]
-    for copy in loads:
+    for copy in loads[:3]:
         copy.start()
 
     def chunk(ref, h, j):
@@ -153,15 +153,8 @@
         src, dst = ((s_chip, s_arr), (cp_chip, cp_arr))[kind]
         return remote(src.at[i], dst.at[slot], in_send.at[kind, i], in_recv.at[kind, slot], device_id)
 
-    def distance(i):
-        ahead = lax.rem(worker_z(i) - z + nz, nz)
-        return jnp.minimum(ahead, nz - ahead)
-
-    farther = jnp.where(distance(0) < distance(pair - 1), pair - 1, 0)
-
     def send_in(kind):
-        for n in range(pair):
-            i = lax.rem(farther + n, pair)
+        for i in range(pair):
             here = z == worker_z(i)
             copy = in_copy(kind, i, z, {"seq_1": worker_z(i)})
 
@@ -195,11 +188,10 @@
                 back_copy(kind, my_head, d).start()
         dst[my_head] = src[z]
 
-    def wait_back(kind):
-        for i in range(pair):
-            @pl.when(z != worker_z(i))
-            def _(i=i):
-                back_copy(kind, i, 1).wait_recv()
+    def wait_back(kind, i):
+        @pl.when(z != worker_z(i))
+        def _():
+            back_copy(kind, i, 1).wait_recv()
 
     def total_copy(kind, d, slot):
         part = (pl.ds(0, 1), pl.ds(1, 2))[kind]
@@ -208,13 +200,26 @@
         )
 
     def send_totals(kind):
-        for d in (2, 1, 3):
+        for d in FAR_FIRST:
             if d < ny:
-                total_copy(kind, d, y).start()
+
+                @pl.when(y + d < ny)
+                def _(d=d):
+                    total_copy(kind, d, y).start()
 
     def wait_totals(kind):
         for d in range(1, ny):
-            total_copy(kind, d, mody(d)).wait_recv()
+
+            @pl.when(y >= d)
+            def _(d=d):
+                total_copy(kind, d, y - d).wait_recv()
+
+    def drain_totals(kind):
+        for d in range(1, ny):
+
+            @pl.when(y + d < ny)
+            def _(d=d):
+                total_copy(kind, d, y).wait_send()
 
     def s_base_until(limit):
         base = jnp.zeros((DH, DH), F32)
@@ -315,6 +320,8 @@
         cp_loc[h // pair, h % pair, 1] = pairs.astype(BF16)
 
     pl.semaphore_wait(barrier, nx - 1 + ny - 1 + 1 + pair - is_worker.astype(jnp.int32))
+    for copy in loads[3:]:
+        copy.start()
     sibling = {"seq_2": 1 - c}
     s_core = remote(s_loc.at[1 - c], s_sib, core_send.at[0], core_recv.at[0], sibling)
     cp_core = remote(cp_loc.at[1 - c], cp_sib, core_send.at[1], core_recv.at[1], sibling)
@@ -383,8 +390,8 @@
             p_back[r] = (p_run[r] + p_base).astype(BF16)
         send_back(1)
 
-    wait_back(0)
     for i in range(pair):
+        wait_back(0, i)
         mine, other = cp_loc[c, i], cp_sib[i]
         chip = s_pre[i]
         early = jnp.where(c == 0, s_loc[c, i], s_sib[i])
@@ -415,43 +422,45 @@
         p_first[h // pair, h % pair] = dot(v_t[h, :, :CHUNK], fs[2 * h], 1, 0)
     relay_x((4, 0), (5, 0), (4, 1), (5, 1))
 
-    wait_back(1)
+    rows_x = tokens // nx
+    loads[4].wait()
+
+    def swap_p(i, slot):
+        return remote(p_other.at[i], p_mine.at[slot, i], core_send.at[3 + i], core_recv.at[3 + i], sibling)
+
+    def head_cols(g, i):
+        return pl.ds(pl.multiple_of(g * (pair * DH) + i * DH, DH), DH)
+
+    def n_copy(d, g, i, slot):
+        cols = head_cols(g, i)
+        number = g * pair + i
+        return remote(
+            n_out.at[d, :, cols], n_in.at[slot, :, cols], n_send.at[d, number], n_recv.at[slot, number], {"head": modx(d)}
+        )
+
     for i in range(pair):
+        wait_back(1, i)
         chip = p_pre[i]
         later = (chip.astype(F32) + p_step[i]).astype(BF16)
         p_mine[c, i] = jnp.where(c == 0, chip, later)
         p_other[i] = jnp.where(c == 0, later, chip)
-    p_swap = remote(p_other, p_mine.at[c], core_send.at[3], core_recv.at[3], sibling)
-    start(p_swap)
-    p_swap_in = remote(p_other, p_mine.at[1 - c], core_send.at[3], core_recv.at[3], sibling)
-
-    rows_x = tokens // nx
-    loads[4].wait()
-
-    def n_copy(d, g, slot):
-        return remote(n_out.at[d, g], n_in.at[slot, g], n_send.at[d, g], n_recv.at[slot, g], {"head": modx(d)})
-
-    for step in range(2):
-        g = c if step == 0 else 1 - c
-        if step == 1:
-            p_swap_in.wait_recv()
-        for i in range(pair):
+        start(swap_p(i, c))
+        for g in (c, 1 - c):
+            if g is not c:
+                swap_p(i, g).wait_recv()
+            cols = head_cols(g, i)
             p_h = p_mine[g, i]
-            p_fin[0, i] = p_h
-            p_fin[1, i] = (p_h.astype(F32) + p_first[g, i]).astype(BF16)
-        for d in (2, 1, 3, 0):
-            target = modx(d)
-            rows = pl.ds(pl.multiple_of(target * rows_x, rows_x), rows_x)
-            part = target // (CHUNK // rows_x)
-            for i in range(pair):
-                cols = pl.ds(pl.multiple_of(g * (pair * DH) + i * DH, DH), DH)
-                attended = o_part[rows, cols] + dot(q[rows, cols], p_fin[part, i], 1, 1)
+            p_fin[0] = p_h
+            p_fin[1] = (p_h.astype(F32) + p_first[g, i]).astype(BF16)
+            for d in (2, 1, 3, 0):
+                target = modx(d)
+                rows = pl.ds(pl.multiple_of(target * rows_x, rows_x), rows_x)
+                part = target // (CHUNK // rows_x)
+                attended = o_part[rows, cols] + dot(q[rows, cols], p_fin[part], 1, 1)
                 mean_square = jnp.mean(attended * attended, axis=-1, keepdims=True)
-                n_out[d, g, :, i * DH : (i + 1) * DH] = (
-                    attended * lax.rsqrt(mean_square + EPS) * gain[:, cols]
-                ).astype(BF16)
-            if d:
-                start(n_copy(d, g, x))
+                n_out[d, :, cols] = (attended * lax.rsqrt(mean_square + EPS) * gain[:, cols]).astype(BF16)
+                if d:
+                    start(n_copy(d, g, i, x))
 
     arrive_plane(2)
     arrive_plane(3)
@@ -460,13 +469,10 @@
     tile = 512
     n_cols = out_ref.shape[1]
 
-    half = w.shape[1] // 2
-
     def project(rows_in, slot, quarter, first, last):
         for begin in range(0, n_cols, tile):
             cols = slice(begin, begin + tile)
-            part = dot(rows_in[slot, 0], w[quarter, :half, cols], 1, 0)
-            part = part + dot(rows_in[slot, 1], w[quarter, half:, cols], 1, 0)
+            part = dot(rows_in[slot], w[quarter, :, cols], 1, 0)
             if not first:
                 part = part + acc[:, cols]
             if last:
@@ -484,8 +490,8 @@
                 core_copy(number, 1 - c).wait_recv()
                 for part in PARTS[number] if number >= 4 else (None,):
                     core_plane_copy(number, part, 1 - c).wait_recv()
-        for g in range(2):
-            n_copy(offset % nx, g, quarter).wait_recv()
+        for head in range(heads):
+            n_copy(offset % nx, head // pair, head % pair, quarter).wait_recv()
         project(n_in, quarter, quarter, False, offset == 2)
 
     for wait in pending:
@@ -498,8 +504,7 @@
         for kind in range(2):
             for d in range(1, nz):
                 back_copy(kind, my_head, d).wait_send()
-            for d in range(1, ny):
-                total_copy(kind, d, y).wait_send()
+            drain_totals(kind)
 
 
 def shards(ny, nz, nx, queries, key_vectors, value_vectors, norm_gain, out_weight):
@@ -550,21 +555,21 @@
             pltpu.VMEM((tokens, width), F32),
             matrices(2, pair, kind=F32),
             pltpu.VMEM((tokens, width), F32),
-            matrices(2, pair),
-            pltpu.VMEM((nx, 2, tokens // nx, width // 2), BF16),
-            pltpu.VMEM((nx, 2, tokens // nx, width // 2), BF16),
+            matrices(2),
+            pltpu.VMEM((nx, tokens // nx, width), BF16),
+            pltpu.VMEM((nx, tokens // nx, width), BF16),
             pltpu.VMEM((tokens // nx, n_cols), F32),
             pltpu.SemaphoreType.DMA((5,)),
-            pltpu.SemaphoreType.DMA((4,)),
-            pltpu.SemaphoreType.DMA((4,)),
+            pltpu.SemaphoreType.DMA((3 + pair,)),
+            pltpu.SemaphoreType.DMA((3 + pair,)),
             pltpu.SemaphoreType.DMA((2, pair)),
             pltpu.SemaphoreType.DMA((2, nz)),
             pltpu.SemaphoreType.DMA((2, nz)),
             pltpu.SemaphoreType.DMA((2, pair)),
             pltpu.SemaphoreType.DMA((2, ny)),
             pltpu.SemaphoreType.DMA((2, ny)),
-            pltpu.SemaphoreType.DMA((nx, 2)),
-            pltpu.SemaphoreType.DMA((nx, 2)),
+            pltpu.SemaphoreType.DMA((nx, heads)),
+            pltpu.SemaphoreType.DMA((nx, heads)),
             pltpu.SemaphoreType.DMA((42,)),
             pltpu.SemaphoreType.DMA((42,)),
         ],

time: 41.9 us -> 40.4 us (0.964)
  Pallas kernels: 41 us -> 39.5 us
    pallas_call x1, Pallas kernels: 41 us -> 39.5 us  [shards(): pl.pallas_call(functools.partial(kernel, ny, nz, nx), out_shape=jax.Shape...]
where the time goes in v7:
time: 40.4 us; the launch traced here: 40.3 us
  Pallas kernels  39.5 us (98%)
  local copies, waits for them, and re-layouts  0.8 us (2%)
    pallas_call x1, Pallas kernels, shards(): pl.pallas_call(functools.partial(kernel, ny, nz, nx), out_shape=jax.Shape...  39.5 us

profile of v7, /device:TPU:1, one launch (start us, length us, event | category | flops | bytes accessed | tf_op | source)
XLA Modules:
  0.0 40.3 jit_solution(15796795914859780310)
XLA Ops:
  0.0 39.5 %shard_map.55 = bf16[128,2048]{1,0:T(8,128)(2,1)S(1)} custom-call(bf16[512,512]{1,0:T(8,128)(2,1)} %q_hbm.1, bf16[512,512]{1,0:T(8,128)(2,1)} %k_hbm.1, bf16[512,512]{1,0:T(8,128)(2,1)} %v_hbm.1, f32[1,512]{1,0:T(1,128)} %bitcast.1, bf16[512,2048]{1,0:T(8,128)(2,1)} %w_hbm.1), custom_call_target="tpu_custom_call" | custom-call | tf_op jit(solution)/shard_map/pallas_call | solution.py:520
  39.5 0.8 %copy.7 = bf16[128,2048]{1,0:T(8,128)(2,1)} copy(bf16[128,2048]{1,0:T(8,128)(2,1)S(1)} %shard_map.55) | data formatting | bytes 1048576

commit v8 on v7

--- a/solution.py
+++ b/solution.py
@@ -153,19 +153,17 @@
         src, dst = ((s_chip, s_arr), (cp_chip, cp_arr))[kind]
         return remote(src.at[i], dst.at[slot], in_send.at[kind, i], in_recv.at[kind, slot], device_id)
 
-    def send_in(kind):
-        for i in range(pair):
-            here = z == worker_z(i)
-            copy = in_copy(kind, i, z, {"seq_1": worker_z(i)})
-
-            @pl.when(jnp.logical_not(here))
-            def _(copy=copy):
-                copy.start()
-
-            @pl.when(here)
-            def _(i=i):
-                src, dst = ((s_chip, s_arr), (cp_chip, cp_arr))[kind]
-                dst[z] = src[i]
+    def send_in(kind, i):
+        here = z == worker_z(i)
+
+        @pl.when(jnp.logical_not(here))
+        def _():
+            in_copy(kind, i, z, {"seq_1": worker_z(i)}).start()
+
+        @pl.when(here)
+        def _():
+            src, dst = ((s_chip, s_arr), (cp_chip, cp_arr))[kind]
+            dst[z] = src[i]
 
     def drain_in(kind):
         for i in range(pair):
@@ -332,15 +330,15 @@
     s_core.wait_recv()
     for i in range(pair):
         s_chip[i] = (s_loc[c, i].astype(F32) + s_sib[i].astype(F32)).astype(BF16)
-    send_in(0)
-    cp_core.wait_recv()
-    for i in range(pair):
+        send_in(0, i)
+        if i == 0:
+            cp_core.wait_recv()
         mine, other = cp_loc[c, i], cp_sib[i]
         early = jnp.where(c == 0, s_loc[c, i], s_sib[i])
         late = jnp.where(c == 0, other[0], mine[0])
         cp_chip[i, 0] = (mine[0].astype(F32) + other[0].astype(F32)).astype(BF16)
         cp_chip[i, 1] = (mine[1].astype(F32) + other[1].astype(F32) + dot(late, early, 1, 0)).astype(BF16)
-    send_in(1)
+        send_in(1, i)
 
     relay_x((0, 0), (1, 0))
 
@@ -390,6 +388,9 @@
             p_back[r] = (p_run[r] + p_base).astype(BF16)
         send_back(1)
 
+    def swap_s(i, slot):
+        return remote(s_other.at[i], s_mine.at[slot, i], core_send.at[2 + i], core_recv.at[2 + i], sibling)
+
     for i in range(pair):
         wait_back(0, i)
         mine, other = cp_loc[c, i], cp_sib[i]
@@ -401,32 +402,33 @@
         p_step[i] = jnp.where(c == 0, mine[1], other[1]).astype(F32) + dot(
             jnp.where(c == 0, mine[0], other[0]), chip, 1, 0
         )
-    s_swap = remote(s_other, s_mine.at[c], core_send.at[2], core_recv.at[2], sibling)
-    start(s_swap)
+        start(swap_s(i, c))
     relay_x((2, None), (3, None))
     arrive_plane(0)
     arrive_plane(1)
-    s_swap_in = remote(s_other, s_mine.at[1 - c], core_send.at[2], core_recv.at[2], sibling)
-    s_swap_in.wait_recv()
-
-    fs = []
-    for h, j in blocks:
-        f = chunk(f_loc, h, j) + dot(chunk(q, h, j), s_mine[h // pair, h % pair], 1, 0)
-        fs.append(f.astype(BF16))
-    mixing = [
-        jnp.where(causal, dot(chunk(q, h, j), fs[n], 1, 1), 0.0).astype(BF16) for n, (h, j) in enumerate(blocks)
-    ]
-    for n, (h, j) in enumerate(blocks):
-        o_part[j * CHUNK : (j + 1) * CHUNK, h * DH : (h + 1) * DH] = dot(mixing[n], chunk(v, h, j), 1, 0)
-    for h in range(heads):
-        p_first[h // pair, h % pair] = dot(v_t[h, :, :CHUNK], fs[2 * h], 1, 0)
-    relay_x((4, 0), (5, 0), (4, 1), (5, 1))
+
+    def local_out(i):
+        both = [(h, j) for h in (i, pair + i) for j in range(2)]
+        fs = []
+        for h, j in both:
+            f = chunk(f_loc, h, j) + dot(chunk(q, h, j), s_mine[h // pair, h % pair], 1, 0)
+            fs.append(f.astype(BF16))
+        mixing = [
+            jnp.where(causal, dot(chunk(q, h, j), fs[n], 1, 1), 0.0).astype(BF16) for n, (h, j) in enumerate(both)
+        ]
+        for n, (h, j) in enumerate(both):
+            o_part[j * CHUNK : (j + 1) * CHUNK, h * DH : (h + 1) * DH] = dot(mixing[n], chunk(v, h, j), 1, 0)
+        for n, h in enumerate((i, pair + i)):
+            p_first[h // pair, h % pair] = dot(v_t[h, :, :CHUNK], fs[2 * n], 1, 0)
+
+    swap_s(0, 1 - c).wait_recv()
+    local_out(0)
 
     rows_x = tokens // nx
     loads[4].wait()
 
     def swap_p(i, slot):
-        return remote(p_other.at[i], p_mine.at[slot, i], core_send.at[3 + i], core_recv.at[3 + i], sibling)
+        return remote(p_other.at[i], p_mine.at[slot, i], core_send.at[2 + pair + i], core_recv.at[2 + pair + i], sibling)
 
     def head_cols(g, i):
         return pl.ds(pl.multiple_of(g * (pair * DH) + i * DH, DH), DH)
@@ -447,6 +449,9 @@
         start(swap_p(i, c))
         for g in (c, 1 - c):
             if g is not c:
+                if i + 1 < pair:
+                    swap_s(i + 1, g).wait_recv()
+                    local_out(i + 1)
                 swap_p(i, g).wait_recv()
             cols = head_cols(g, i)
             p_h = p_mine[g, i]
@@ -461,6 +466,8 @@
                 n_out[d, :, cols] = (attended * lax.rsqrt(mean_square + EPS) * gain[:, cols]).astype(BF16)
                 if d:
                     start(n_copy(d, g, i, x))
+        if i == 0:
+            relay_x((4, 0), (5, 0), (4, 1), (5, 1))
 
     arrive_plane(2)
     arrive_plane(3)
@@ -560,8 +567,8 @@
             pltpu.VMEM((nx, tokens // nx, width), BF16),
             pltpu.VMEM((tokens // nx, n_cols), F32),
             pltpu.SemaphoreType.DMA((5,)),
-            pltpu.SemaphoreType.DMA((3 + pair,)),
-            pltpu.SemaphoreType.DMA((3 + pair,)),
+            pltpu.SemaphoreType.DMA((2 + 2 * pair,)),
+            pltpu.SemaphoreType.DMA((2 + 2 * pair,)),
             pltpu.SemaphoreType.DMA((2, pair)),
             pltpu.SemaphoreType.DMA((2, nz)),
             pltpu.SemaphoreType.DMA((2, nz)),

time: 40.4 us -> 41.3 us (1.022)
  Pallas kernels: 39.5 us -> 40.4 us
    pallas_call x1, Pallas kernels: 39.5 us -> 40.4 us  [shards(): pl.pallas_call(functools.partial(kernel, ny, nz, nx), out_shape=jax.Shape...]
where the time goes in v8:
time: 41.3 us; the launch traced here: 41.2 us
  Pallas kernels  40.4 us (98%)
  local copies, waits for them, and re-layouts  0.8 us (2%)
    pallas_call x1, Pallas kernels, shards(): pl.pallas_call(functools.partial(kernel, ny, nz, nx), out_shape=jax.Shape...  40.4 us

profile of v8, /device:TPU:1, one launch (start us, length us, event | category | flops | bytes accessed | tf_op | source)
XLA Modules:
  0.0 41.2 jit_solution(10978337708465761485)
XLA Ops:
  0.0 40.4 %shard_map.55 = bf16[128,2048]{1,0:T(8,128)(2,1)S(1)} custom-call(bf16[512,512]{1,0:T(8,128)(2,1)} %q_hbm.1, bf16[512,512]{1,0:T(8,128)(2,1)} %k_hbm.1, bf16[512,512]{1,0:T(8,128)(2,1)} %v_hbm.1, f32[1,512]{1,0:T(1,128)} %bitcast.1, bf16[512,2048]{1,0:T(8,128)(2,1)} %w_hbm.1), custom_call_target="tpu_custom_call" | custom-call | tf_op jit(solution)/shard_map/pallas_call | solution.py:527
  40.4 0.8 %copy.7 = bf16[128,2048]{1,0:T(8,128)(2,1)} copy(bf16[128,2048]{1,0:T(8,128)(2,1)S(1)} %shard_map.55) | data formatting | bytes 1048576

commit v9 on v7

--- a/solution.py
+++ b/solution.py
@@ -130,6 +130,12 @@
         greet({"head": modx(d)})
     greet({"seq_2": 1 - c})
 
+    is_first = (y == 0) & (z == 0)
+
+    @pl.when((y == 0) & ((z == 1) | (z == nz - 1)))
+    def _():
+        greet({"seq_1": 0})
+
     @pl.when(is_worker)
     def _():
         for d in FAR_FIRST:
@@ -177,21 +183,34 @@
         for d in range(1, nz):
             in_copy(kind, 0, modz(d), {"seq_1": modz(d)}).wait_recv()
 
-    def back_copy(kind, i, d):
+    def back_copy(kind, i, t):
         src, dst = ((s_back, s_pre), (p_back, p_pre))[kind]
-        return remote(src.at[modz(d)], dst.at[i], back_send.at[kind, d], back_recv.at[kind, i], {"seq_1": modz(d)})
+        return remote(src.at[t], dst.at[i], back_send.at[kind, t], back_recv.at[kind, i], {"seq_1": t})
+
+    def takes_back(t):
+        return (z != t) & (y > 0) if t == 0 else z != t
 
     def send_back(kind):
+        for t in range(nz):
+
+            @pl.when(takes_back(t))
+            def _(t=t):
+                back_copy(kind, my_head, t).start()
+
         src, dst = ((s_back, s_pre), (p_back, p_pre))[kind]
-        for d in FAR_FIRST:
-            if d < nz:
-                back_copy(kind, my_head, d).start()
         dst[my_head] = src[z]
 
+    def drain_back(kind):
+        for t in range(nz):
+
+            @pl.when(takes_back(t))
+            def _(t=t):
+                back_copy(kind, my_head, t).wait_send()
+
     def wait_back(kind, i):
-        @pl.when(z != worker_z(i))
+        @pl.when((z != worker_z(i)) & jnp.logical_not(is_first))
         def _():
-            back_copy(kind, i, 1).wait_recv()
+            back_copy(kind, i, 0).wait_recv()
 
     def total_copy(kind, d, slot):
         part = (pl.ds(0, 1), pl.ds(1, 2))[kind]
@@ -319,7 +338,7 @@
         cp_loc[h // pair, h % pair, 0] = cross.astype(BF16)
         cp_loc[h // pair, h % pair, 1] = pairs.astype(BF16)
 
-    pl.semaphore_wait(barrier, nx - 1 + ny - 1 + 1 + pair - is_worker.astype(jnp.int32))
+    pl.semaphore_wait(barrier, nx - 1 + ny - 1 + 1 + pair - is_worker.astype(jnp.int32) + 2 * is_first.astype(jnp.int32))
     for copy in loads[3:]:
         copy.start()
     sibling = {"seq_2": 1 - c}
@@ -341,6 +360,39 @@
         cp_chip[i, 0] = (mine[0].astype(F32) + other[0].astype(F32)).astype(BF16)
         cp_chip[i, 1] = (mine[1].astype(F32) + other[1].astype(F32) + dot(late, early, 1, 0)).astype(BF16)
     send_in(1)
+
+    def by_core(i):
+        own, other = cp_loc[c, i], cp_sib[i]
+        return jnp.where(c == 0, s_loc[c, i], s_sib[i]), jnp.where(c == 0, own[0], other[0]), jnp.where(c == 0, own[1], other[1])
+
+    def s_before_core(i, chip):
+        s_early, c_early, p_early = by_core(i)
+        later = (chip.astype(F32) + s_early.astype(F32)).astype(BF16)
+        s_mine[c, i] = jnp.where(c == 0, chip, later)
+        s_other[i] = jnp.where(c == 0, later, chip)
+        p_step[i] = p_early.astype(F32) + dot(c_early, chip, 1, 0)
+
+    def p_before_core(i, chip):
+        later = (chip.astype(F32) + p_step[i]).astype(BF16)
+        p_mine[c, i] = jnp.where(c == 0, chip, later)
+        p_other[i] = jnp.where(c == 0, later, chip)
+
+    swap_s = remote(s_other, s_mine.at[c], core_send.at[2], core_recv.at[2], sibling)
+
+    def swap_p(i, slot):
+        return remote(p_other.at[i], p_mine.at[slot, i], core_send.at[3 + i], core_recv.at[3 + i], sibling)
+
+    swaps_p = [swap_p(i, c) for i in range(pair)]
+
+    @pl.when(is_first)
+    def _():
+        nothing = jnp.zeros((DH, DH), BF16)
+        for i in range(pair):
+            s_before_core(i, nothing)
+            p_before_core(i, nothing)
+        swap_s.start()
+        for copy in swaps_p:
+            copy.start()
 
     relay_x((0, 0), (1, 0))
 
@@ -392,22 +444,18 @@
 
     for i in range(pair):
         wait_back(0, i)
-        mine, other = cp_loc[c, i], cp_sib[i]
-        chip = s_pre[i]
-        early = jnp.where(c == 0, s_loc[c, i], s_sib[i])
-        later = (chip.astype(F32) + early.astype(F32)).astype(BF16)
-        s_mine[c, i] = jnp.where(c == 0, chip, later)
-        s_other[i] = jnp.where(c == 0, later, chip)
-        p_step[i] = jnp.where(c == 0, mine[1], other[1]).astype(F32) + dot(
-            jnp.where(c == 0, mine[0], other[0]), chip, 1, 0
-        )
-    s_swap = remote(s_other, s_mine.at[c], core_send.at[2], core_recv.at[2], sibling)
-    start(s_swap)
+
+    @pl.when(jnp.logical_not(is_first))
+    def _():
+        for i in range(pair):
+            s_before_core(i, s_pre[i])
+        swap_s.start()
+
+    pending.append(swap_s.wait_send)
     relay_x((2, None), (3, None))
     arrive_plane(0)
     arrive_plane(1)
-    s_swap_in = remote(s_other, s_mine.at[1 - c], core_send.at[2], core_recv.at[2], sibling)
-    s_swap_in.wait_recv()
+    remote(s_other, s_mine.at[1 - c], core_send.at[2], core_recv.at[2], sibling).wait_recv()
 
     fs = []
     for h, j in blocks:
@@ -425,9 +473,6 @@
     rows_x = tokens // nx
     loads[4].wait()
 
-    def swap_p(i, slot):
-        return remote(p_other.at[i], p_mine.at[slot, i], core_send.at[3 + i], core_recv.at[3 + i], sibling)
-
     def head_cols(g, i):
         return pl.ds(pl.multiple_of(g * (pair * DH) + i * DH, DH), DH)
 
@@ -440,11 +485,13 @@
 
     for i in range(pair):
         wait_back(1, i)
-        chip = p_pre[i]
-        later = (chip.astype(F32) + p_step[i]).astype(BF16)
-        p_mine[c, i] = jnp.where(c == 0, chip, later)
-        p_other[i] = jnp.where(c == 0, later, chip)
-        start(swap_p(i, c))
+
+        @pl.when(jnp.logical_not(is_first))
+        def _(i=i):
+            p_before_core(i, p_pre[i])
+            swaps_p[i].start()
+
+        pending.append(swaps_p[i].wait_send)
         for g in (c, 1 - c):
             if g is not c:
                 swap_p(i, g).wait_recv()
@@ -502,8 +549,7 @@
     @pl.when(is_worker)
     def _():
         for kind in range(2):
-            for d in range(1, nz):
-                back_copy(kind, my_head, d).wait_send()
+            drain_back(kind)
             drain_totals(kind)
 
 

time: 40.4 us -> 40.3 us (level)
  no operation moved by 1% of the time
where the time goes in v9:
time: 40.3 us; the launch traced here: 40.2 us
  Pallas kernels  39.4 us (98%)
  local copies, waits for them, and re-layouts  0.8 us (2%)
    pallas_call x1, Pallas kernels, shards(): pl.pallas_call(functools.partial(kernel, ny, nz, nx), out_shape=jax.Shape...  39.4 us

profile of v9, /device:TPU:1, one launch (start us, length us, event | category | flops | bytes accessed | tf_op | source)
XLA Modules:
  0.0 40.2 jit_solution(17399898154454602390)
XLA Ops:
  0.0 39.4 %shard_map.55 = bf16[128,2048]{1,0:T(8,128)(2,1)S(1)} custom-call(bf16[512,512]{1,0:T(8,128)(2,1)} %q_hbm.1, bf16[512,512]{1,0:T(8,128)(2,1)} %k_hbm.1, bf16[512,512]{1,0:T(8,128)(2,1)} %v_hbm.1, f32[1,512]{1,0:T(1,128)} %bitcast.1, bf16[512,2048]{1,0:T(8,128)(2,1)} %w_hbm.1), custom_call_target="tpu_custom_call" | custom-call | tf_op jit(solution)/shard_map/pallas_call | solution.py:566
  39.5 0.8 %copy.7 = bf16[128,2048]{1,0:T(8,128)(2,1)} copy(bf16[128,2048]{1,0:T(8,128)(2,1)S(1)} %shard_map.55) | data formatting | bytes 1048576

commit v10 on v9

--- a/solution.py
+++ b/solution.py
@@ -282,7 +282,7 @@
     def plane_copy(number, part, colour_of):
         ref = piece(number, colour_of, c, part)
         step = 1 if X_PIECES[number][1] == 0 else -1
-        peer = {"seq_1": modz(step + nz)} if number >= 4 and part == 1 else {"seq_0": mody(step)}
+        peer = {"seq_1": modz(step + nz)} if number >= 4 else {"seq_0": mody(step)}
         return w_copy(12 + unit(number, part), ref, ref, peer)
 
     def core_copy(number, core_of):

time: 40.3 us -> 39.8 us (0.988)
  Pallas kernels: 39.4 us -> 38.9 us
    pallas_call x1, Pallas kernels: 39.4 us -> 38.9 us  [shards(): pl.pallas_call(functools.partial(kernel, ny, nz, nx), out_shape=jax.Shape...]
where the time goes in v10:
time: 39.8 us; the launch traced here: 39.7 us
  Pallas kernels  38.9 us (98%)
  local copies, waits for them, and re-layouts  0.8 us (2%)
    pallas_call x1, Pallas kernels, shards(): pl.pallas_call(functools.partial(kernel, ny, nz, nx), out_shape=jax.Shape...  38.9 us

profile of v10, /device:TPU:1, one launch (start us, length us, event | category | flops | bytes accessed | tf_op | source)
XLA Modules:
  0.0 39.7 jit_solution(13917366470928648966)
XLA Ops:
  0.0 38.9 %shard_map.55 = bf16[128,2048]{1,0:T(8,128)(2,1)S(1)} custom-call(bf16[512,512]{1,0:T(8,128)(2,1)} %q_hbm.1, bf16[512,512]{1,0:T(8,128)(2,1)} %k_hbm.1, bf16[512,512]{1,0:T(8,128)(2,1)} %v_hbm.1, f32[1,512]{1,0:T(1,128)} %bitcast.1, bf16[512,2048]{1,0:T(8,128)(2,1)} %w_hbm.1), custom_call_target="tpu_custom_call" | custom-call | tf_op jit(solution)/shard_map/pallas_call | solution.py:566
  38.9 0.8 %copy.7 = bf16[128,2048]{1,0:T(8,128)(2,1)} copy(bf16[128,2048]{1,0:T(8,128)(2,1)S(1)} %shard_map.55) | data formatting | bytes 1048576

commit v11 on v10

--- a/solution.py
+++ b/solution.py
@@ -306,10 +306,13 @@
     def arrive_plane(number):
         for part in PARTS[number]:
             plane_copy(number, part, 1 - colour).wait_recv()
-            if number >= 4:
+        start(core_plane_copy(number, None, c))
+
+    def arrive_last():
+        for part in range(2):
+            for number in (5, 4):
+                plane_copy(number, part, 1 - colour).wait_recv()
                 start(core_plane_copy(number, part, c))
-        if number < 4:
-            start(core_plane_copy(number, None, c))
 
     row = lax.broadcasted_iota(jnp.int32, (CHUNK, CHUNK), 0)
     col = lax.broadcasted_iota(jnp.int32, (CHUNK, CHUNK), 1)
@@ -325,6 +328,16 @@
     for h in range(heads):
         v_t[h] = v[:, h * DH : (h + 1) * DH].T
     scores = [jnp.where(strict, dot(chunk(q, h, j), chunk(k, h, j), 1, 1), 0.0).astype(BF16) for h, j in blocks]
+    pl.semaphore_wait(barrier, nx - 1 + ny - 1 + 1 + pair - is_worker.astype(jnp.int32) + 2 * is_first.astype(jnp.int32))
+    for copy in loads[3:]:
+        copy.start()
+    sibling = {"seq_2": 1 - c}
+    s_core = remote(s_loc.at[1 - c], s_sib, core_send.at[0], core_recv.at[0], sibling)
+    cp_core = remote(cp_loc.at[1 - c], cp_sib, core_send.at[1], core_recv.at[1], sibling)
+    start(s_core)
+    for number, part in ((0, 0), (1, 0), (0, 1), (1, 1), (2, None), (3, None)):
+        start(x_send(number, part))
+
     fs = []
     for n, (h, j) in enumerate(blocks):
         f = dot(scores[n], chunk(k, h, j), 1, 0)
@@ -338,16 +351,7 @@
         cp_loc[h // pair, h % pair, 0] = cross.astype(BF16)
         cp_loc[h // pair, h % pair, 1] = pairs.astype(BF16)
 
-    pl.semaphore_wait(barrier, nx - 1 + ny - 1 + 1 + pair - is_worker.astype(jnp.int32) + 2 * is_first.astype(jnp.int32))
-    for copy in loads[3:]:
-        copy.start()
-    sibling = {"seq_2": 1 - c}
-    s_core = remote(s_loc.at[1 - c], s_sib, core_send.at[0], core_recv.at[0], sibling)
-    cp_core = remote(cp_loc.at[1 - c], cp_sib, core_send.at[1], core_recv.at[1], sibling)
-    start(s_core)
     start(cp_core)
-    for number, part in ((0, 0), (1, 0), (0, 1), (1, 1), (2, None), (3, None)):
-        start(x_send(number, part))
     s_core.wait_recv()
     for i in range(pair):
         s_chip[i] = (s_loc[c, i].astype(F32) + s_sib[i].astype(F32)).astype(BF16)
@@ -509,9 +513,6 @@
                 if d:
                     start(n_copy(d, g, i, x))
 
-    arrive_plane(2)
-    arrive_plane(3)
-
     loads[3].wait()
     tile = 512
     n_cols = out_ref.shape[1]
@@ -528,8 +529,9 @@
                 acc[:, cols] = part
 
     project(n_out, 0, x, True, False)
-    arrive_plane(4)
-    arrive_plane(5)
+    arrive_plane(2)
+    arrive_plane(3)
+    arrive_last()
     for offset in (-1, 1, 2):
         quarter = modx(offset)
         for number, (of, _) in enumerate(X_PIECES):

time: 39.8 us -> 39.8 us (level)
  no operation moved by 1% of the time
where the time goes in v11:
time: 39.8 us; the launch traced here: 39.7 us
  Pallas kernels  38.9 us (98%)
  local copies, waits for them, and re-layouts  0.8 us (2%)
    pallas_call x1, Pallas kernels, shards(): pl.pallas_call(functools.partial(kernel, ny, nz, nx), out_shape=jax.Shape...  38.9 us

profile of v11, /device:TPU:1, one launch (start us, length us, event | category | flops | bytes accessed | tf_op | source)
XLA Modules:
  0.0 39.7 jit_solution(17488313012784389252)
XLA Ops:
  0.0 38.9 %shard_map.55 = bf16[128,2048]{1,0:T(8,128)(2,1)S(1)} custom-call(bf16[512,512]{1,0:T(8,128)(2,1)} %q_hbm.1, bf16[512,512]{1,0:T(8,128)(2,1)} %k_hbm.1, bf16[512,512]{1,0:T(8,128)(2,1)} %v_hbm.1, f32[1,512]{1,0:T(1,128)} %bitcast.1, bf16[512,2048]{1,0:T(8,128)(2,1)} %w_hbm.1), custom_call_target="tpu_custom_call" | custom-call | tf_op jit(solution)/shard_map/pallas_call | solution.py:568
  38.9 0.8 %copy.7 = bf16[128,2048]{1,0:T(8,128)(2,1)} copy(bf16[128,2048]{1,0:T(8,128)(2,1)S(1)} %shard_map.55) | data formatting | bytes 1048576

commit v12 on v11

--- a/solution.py
+++ b/solution.py
@@ -285,6 +285,34 @@
         peer = {"seq_1": modz(step + nz)} if number >= 4 else {"seq_0": mody(step)}
         return w_copy(12 + unit(number, part), ref, ref, peer)
 
+    def block_copy(n, colour_of, over_y=False):
+        first = colour_of * (4 * piece_rows) + c * (2 * piece_rows) + piece_rows // 2 + n * (piece_rows // 4)
+        ref = w.at[modx(2), pl.ds(pl.multiple_of(first, piece_rows // 4), piece_rows // 4)]
+        if over_y:
+            return remote(ref, ref, w_send.at[43], w_recv.at[12 + unit(4, 1)], {"seq_0": mody(-1)})
+        return w_copy((12 + unit(4, 1), 42)[n], ref, ref, {"seq_1": modz(1)})
+
+    def send_blocks():
+        @pl.when(z == 0)
+        def _():
+            block_copy(0, colour, True).start()
+
+        @pl.when(z != nz - 1)
+        def _():
+            block_copy(0, colour).start()
+
+        start(block_copy(1, colour))
+        pending.append(drain_blocks)
+
+    def drain_blocks():
+        @pl.when(z == 0)
+        def _():
+            block_copy(0, colour, True).wait_send()
+
+        @pl.when(z != nz - 1)
+        def _():
+            block_copy(0, colour).wait_send()
+
     def core_copy(number, core_of):
         ref = piece(number, colour, core_of)
         return w_copy(24 + number, ref, ref, {"seq_2": 1 - c})
@@ -298,7 +326,10 @@
             x_arrival(number, part).wait_recv()
             if number < 2:
                 start(x_send(4 + number, part))
-            start(plane_copy(number, part, colour))
+            if (number, part) == (4, 1):
+                send_blocks()
+            else:
+                start(plane_copy(number, part, colour))
         for number, part in units:
             if part != 0:
                 start(core_copy(number, c))
@@ -311,7 +342,11 @@
     def arrive_last():
         for part in range(2):
             for number in (5, 4):
-                plane_copy(number, part, 1 - colour).wait_recv()
+                if (number, part) == (4, 1):
+                    block_copy(0, 1 - colour).wait_recv()
+                    block_copy(1, 1 - colour).wait_recv()
+                else:
+                    plane_copy(number, part, 1 - colour).wait_recv()
                 start(core_plane_copy(number, part, c))
 
     row = lax.broadcasted_iota(jnp.int32, (CHUNK, CHUNK), 0)
@@ -618,8 +653,8 @@
             pltpu.SemaphoreType.DMA((2, ny)),
             pltpu.SemaphoreType.DMA((nx, heads)),
             pltpu.SemaphoreType.DMA((nx, heads)),
-            pltpu.SemaphoreType.DMA((42,)),
-            pltpu.SemaphoreType.DMA((42,)),
+            pltpu.SemaphoreType.DMA((44,)),
+            pltpu.SemaphoreType.DMA((44,)),
         ],
         compiler_params=pltpu.CompilerParams(
             collective_id=0, has_side_effects=True, vmem_limit_bytes=48 * 1024 * 1024

time: 39.8 us -> 39.8 us (level)
  no operation moved by 1% of the time
where the time goes in v12:
time: 39.8 us; the launch traced here: 39.7 us
  Pallas kernels  38.9 us (98%)
  local copies, waits for them, and re-layouts  0.8 us (2%)
    pallas_call x1, Pallas kernels, shards(): pl.pallas_call(functools.partial(kernel, ny, nz, nx), out_shape=jax.Shape...  38.9 us

profile of v12, /device:TPU:1, one launch (start us, length us, event | category | flops | bytes accessed | tf_op | source)
XLA Modules:
  0.0 39.7 jit_solution(16029798006199854615)
XLA Ops:
  0.0 38.9 %shard_map.55 = bf16[128,2048]{1,0:T(8,128)(2,1)S(1)} custom-call(bf16[512,512]{1,0:T(8,128)(2,1)} %q_hbm.1, bf16[512,512]{1,0:T(8,128)(2,1)} %k_hbm.1, bf16[512,512]{1,0:T(8,128)(2,1)} %v_hbm.1, f32[1,512]{1,0:T(1,128)} %bitcast.1, bf16[512,2048]{1,0:T(8,128)(2,1)} %w_hbm.1), custom_call_target="tpu_custom_call" | custom-call | tf_op jit(solution)/shard_map/pallas_call | solution.py:603
  38.9 0.8 %copy.7 = bf16[128,2048]{1,0:T(8,128)(2,1)} copy(bf16[128,2048]{1,0:T(8,128)(2,1)S(1)} %shard_map.55) | data formatting | bytes 1048576

commit v13 on v12

--- a/solution.py
+++ b/solution.py
@@ -481,6 +481,11 @@
             p_back[r] = (p_run[r] + p_base).astype(BF16)
         send_back(1)
 
+    @pl.when(y == ny - 1)
+    def _():
+        x_arrival(3, None).wait_recv()
+        plane_copy(3, None, colour).start()
+
     for i in range(pair):
         wait_back(0, i)
 
@@ -491,7 +496,15 @@
         swap_s.start()
 
     pending.append(swap_s.wait_send)
-    relay_x((2, None), (3, None))
+    relay_x((2, None))
+
+    @pl.when(y != ny - 1)
+    def _():
+        x_arrival(3, None).wait_recv()
+        plane_copy(3, None, colour).start()
+
+    pending.append(plane_copy(3, None, colour).wait_send)
+    start(core_copy(3, c))
     arrive_plane(0)
     arrive_plane(1)
     remote(s_other, s_mine.at[1 - c], core_send.at[2], core_recv.at[2], sibling).wait_recv()

time: 39.8 us -> 39.8 us (level)
  no operation moved by 1% of the time
where the time goes in v13:
time: 39.8 us; the launch traced here: 39.7 us
  Pallas kernels  38.9 us (98%)
  local copies, waits for them, and re-layouts  0.8 us (2%)
    pallas_call x1, Pallas kernels, shards(): pl.pallas_call(functools.partial(kernel, ny, nz, nx), out_shape=jax.Shape...  38.9 us

profile of v13, /device:TPU:1, one launch (start us, length us, event | category | flops | bytes accessed | tf_op | source)
XLA Modules:
  0.0 39.7 jit_solution(4998136370292383948)
XLA Ops:
  0.0 38.9 %shard_map.55 = bf16[128,2048]{1,0:T(8,128)(2,1)S(1)} custom-call(bf16[512,512]{1,0:T(8,128)(2,1)} %q_hbm.1, bf16[512,512]{1,0:T(8,128)(2,1)} %k_hbm.1, bf16[512,512]{1,0:T(8,128)(2,1)} %v_hbm.1, f32[1,512]{1,0:T(1,128)} %bitcast.1, bf16[512,2048]{1,0:T(8,128)(2,1)} %w_hbm.1), custom_call_target="tpu_custom_call" | custom-call | tf_op jit(solution)/shard_map/pallas_call | solution.py:616
  38.9 0.8 %copy.7 = bf16[128,2048]{1,0:T(8,128)(2,1)} copy(bf16[128,2048]{1,0:T(8,128)(2,1)S(1)} %shard_map.55) | data formatting | bytes 1048576
